TPU v7x, 32 devices: a whole 2x2x4 slice. The times are simulated.
32 devices in a mesh: grp: 4 (over y, core), mem: 8 (over z, x).
Axes of the slice: x: 2, y: 2, z: 4, core: 2. Of those that a mesh axis runs over, the one named last changes fastest.
Arguments:
- coefficients: float32 [8, 240, 4096], P(None, None, ('grp', 'mem')), may hold values from -6 to 6
- incident: float32 [8, 240, 4096], P(None, None, ('grp', 'mem')), may hold values from -6 to 6
- mie_coeffs: float32 [2, 240], replicated, may hold values from -0.8 to 0.8
- rot_table: bfloat16 [8, 240, 240], replicated, may hold values from -0.375 to 0.375
- axial_shells: bfloat16 [3, 2, 240, 240], replicated, may hold values from -0.1875 to 0.1875
- up_axial: bfloat16 [2, 240, 240], replicated, may hold values from -0.1875 to 0.1875
- far_axial: bfloat16 [2, 240, 240], replicated, may hold values from -0.0625 to 0.0625
- coupling: float32 [64, 64], replicated, may hold values from 0.01 to 0.1
- cluster_ids: int32 [4096], P(('grp', 'mem')), may hold values from 0 to 15
- center_rot: int32 [4096], P(('grp', 'mem')), may hold values from 0 to 7
- pair_col: int32 [24, 4096], P(None, ('grp', 'mem')), may hold values from -1 to 1407, as said below
- pair_rot: int32 [24, 4096], P(None, ('grp', 'mem')), may hold values from -1 to 7, as said below
- send_col: int32 [192, 64], P(('grp', 'mem')), may hold values from 0 to 1023, as said below
Outputs:
- updated: float32 [8, 240, 4096], P(None, None, ('grp', 'mem'))
Inputs may be any that keep to these rules, and one draw needn't show every extreme that they name: `pair_col`: -1 marks an empty slot; a value below 1024 is r * 128 + j for the own device's sphere j rotated by entry r; a larger one is 1024 + p * 64 + c for the c-th column sent to this device by its neighbour p; every such received column is named by some slot of the receiving device. `pair_rot`: -1 exactly in empty slots; otherwise the table entry with which the slot's column was rotated. `send_col`: row d * 6 + p lists the pool columns r * 128 + j that device d provides to the device whose neighbour p it is.
All inputs are finite; a program needn't handle non-finite values.
Results may differ from a plain program's by a relative error of at most 0.0038.
The roundings to bfloat16 on the way count: a program that leaves them out, or rounds other values in their place, can miss the bound.
Values may be sent and summed in bfloat16 or wider, within the bound.
A program may use at most 128 MiB of HBM per device.

v0:
```python
import jax
import jax.numpy as jnp
from jax import lax
from jax.sharding import PartitionSpec as P


def shifted(value, axis, by):
    length = lax.axis_size(axis)
    return lax.ppermute(value, axis, [(i, (i + by) % length) for i in range(length)])


def complex_apply(matrix_pair, columns):
    dir_count = columns.shape[1] // 2
    real_in = columns[:, :dir_count]
    imag_in = columns[:, dir_count:]
    real_out = jnp.einsum(
        "kc,cxn->kxn", matrix_pair[0], real_in, preferred_element_type=jnp.float32
    ) - jnp.einsum("kc,cxn->kxn", matrix_pair[1], imag_in, preferred_element_type=jnp.float32)
    imag_out = jnp.einsum(
        "kc,cxn->kxn", matrix_pair[0], imag_in, preferred_element_type=jnp.float32
    ) + jnp.einsum("kc,cxn->kxn", matrix_pair[1], real_in, preferred_element_type=jnp.float32)
    return jnp.concatenate([real_out, imag_out], axis=1)


def pool_select(rotated, column_ids, sph_count):
    rot_count = rotated.shape[0]
    flat_ids = column_ids.reshape(-1)
    rot_iota = jnp.arange(rot_count, dtype=jnp.int32)
    sph_iota = jnp.arange(sph_count, dtype=jnp.int32)
    valid = (flat_ids >= 0) & (flat_ids < rot_count * sph_count)
    match_rot = (flat_ids // sph_count)[None, None, :] == rot_iota[:, None, None]
    match_sph = (flat_ids % sph_count)[None, None, :] == sph_iota[None, :, None]
    selector = (match_rot & match_sph & valid[None, None, :]).astype(jnp.bfloat16)
    return jnp.einsum("rkxn,rnm->kxm", rotated, selector, preferred_element_type=jnp.float32)


def on_device(
    coefficients,
    incident,
    mie_coeffs,
    rot_table,
    axial_shells,
    up_axial,
    far_axial,
    coupling,
    cluster_ids,
    center_rot,
    pair_col,
    pair_rot,
    send_col,
):
    highest = lax.Precision.HIGHEST
    comps, n_coef, sph_count = coefficients.shape
    rot_count = rot_table.shape[0]
    pool_size = rot_count * sph_count
    group_count = lax.axis_size("grp")
    clus_total = coupling.shape[0]
    clus_group = clus_total // group_count
    sph_iota = jnp.arange(sph_count, dtype=jnp.int32)
    peer_count, width = send_col.shape
    mem_moves = [1, -1, 2, -2]
    grp_moves = [1, -1]
    coef_major = jnp.transpose(coefficients.astype(jnp.bfloat16), (1, 0, 2))
    rotated = jnp.einsum(
        "rkc,cxn->rkxn", rot_table, coef_major, preferred_element_type=jnp.float32
    ).astype(jnp.bfloat16)
    outgoing = (
        pool_select(rotated, send_col, sph_count)
        .astype(jnp.bfloat16)
        .reshape(n_coef, comps, peer_count, width)
    )
    received = []
    for peer_idx in range(len(mem_moves)):
        received.append(shifted(outgoing[:, :, peer_idx], "mem", mem_moves[peer_idx]))
    for grp_idx in range(len(grp_moves)):
        peer_idx = len(mem_moves) + grp_idx
        received.append(shifted(outgoing[:, :, peer_idx], "grp", grp_moves[grp_idx]))
    arrived = jnp.concatenate(received, axis=2)
    recv_size = arrived.shape[2]
    own_ids = center_rot * sph_count + sph_iota
    picked = pool_select(rotated, own_ids, sph_count).astype(jnp.bfloat16)
    lifted = complex_apply(up_axial, picked)
    member_onehot = (
        cluster_ids[:, None] == jnp.arange(clus_group, dtype=jnp.int32)[None, :]
    ).astype(jnp.float32)
    partial_exp = jnp.einsum("kxn,nc->kxc", lifted, member_onehot, precision=highest)
    row_start = lax.axis_index("grp") * clus_group
    shares = lax.psum_scatter(partial_exp, "mem", scatter_dimension=2, tiled=True)
    expansions = lax.all_gather(shares, ("grp", "mem"), axis=2, tiled=True)
    coupling_rows = lax.dynamic_slice_in_dim(coupling, row_start, clus_group, 0)
    row_ids = row_start + jnp.arange(clus_group, dtype=jnp.int32)
    col_ids = jnp.arange(clus_total, dtype=jnp.int32)
    coupling_rows = jnp.where(row_ids[:, None] == col_ids[None, :], jnp.float32(0.0), coupling_rows)
    reached = jnp.einsum("cd,kxd->kxc", coupling_rows, expansions, precision=highest)
    far_local = complex_apply(far_axial, reached.astype(jnp.bfloat16))
    far_each = jnp.einsum("kxc,nc->kxn", far_local, member_onehot, precision=highest)
    shell_count = axial_shells.shape[0]
    per_shell = pair_col.shape[0] // shell_count
    recv_iota = jnp.arange(recv_size, dtype=jnp.int32)
    partial_rot = [
        jnp.where((center_rot == rot_idx)[None, None, :], far_each, jnp.float32(0.0))
        for rot_idx in range(rot_count)
    ]
    for shell_idx in range(shell_count):
        slot_cols = pair_col[shell_idx * per_shell : (shell_idx + 1) * per_shell]
        slot_rots = pair_rot[shell_idx * per_shell : (shell_idx + 1) * per_shell]
        own_part = pool_select(rotated, slot_cols, sph_count)
        recv_select = ((slot_cols.reshape(-1) - pool_size)[None, :] == recv_iota[:, None]).astype(
            jnp.bfloat16
        )
        recv_part = jnp.einsum(
            "kxa,am->kxm", arrived, recv_select, preferred_element_type=jnp.float32
        )
        taken = (own_part + recv_part).astype(jnp.bfloat16)
        moved = complex_apply(axial_shells[shell_idx], taken).reshape(
            n_coef, comps, per_shell, sph_count
        )
        for rot_idx in range(rot_count):
            chosen = jnp.where((slot_rots == rot_idx)[None, None], moved, jnp.float32(0.0))
            partial_rot[rot_idx] = partial_rot[rot_idx] + jnp.sum(chosen, axis=2)
    totals = jnp.stack(partial_rot, axis=0).astype(jnp.bfloat16)
    field_major = jnp.einsum("rck,rcxn->kxn", rot_table, totals, preferred_element_type=jnp.float32)
    field = jnp.transpose(field_major, (1, 0, 2))
    summed = incident + field
    dir_count = comps // 2
    real_part = summed[:dir_count]
    imag_part = summed[dir_count:]
    mie_real = mie_coeffs[0][None, :, None]
    mie_imag = mie_coeffs[1][None, :, None]
    return jnp.concatenate(
        [mie_real * real_part - mie_imag * imag_part, mie_real * imag_part + mie_imag * real_part],
        axis=0,
    )


def solution(mesh):
    in_specs = (
        P(None, None, ("grp", "mem")),
        P(None, None, ("grp", "mem")),
        P(),
        P(),
        P(),
        P(),
        P(),
        P(),
        P(("grp", "mem")),
        P(("grp", "mem")),
        P(None, ("grp", "mem")),
        P(None, ("grp", "mem")),
        P(("grp", "mem"), None),
    )
    out_specs = P(None, None, ("grp", "mem"))
    return jax.shard_map(
        on_device, mesh=mesh, in_specs=in_specs, out_specs=out_specs, check_vma=False
    )
```

profile of v0, /device:TPU:0, one launch (start us, length us, event | category | flops | bytes accessed | tf_op | source)
XLA Modules:
  0.0 344.3 jit_solution(4403085618567399125)
XLA Ops:
  6.5 0.8 reshape.559
  7.8 2.4 convolution_convert_fusion
  10.2 1.9 copy-done.1
  12.0 4.0 %bitcast_convert_fusion = bf16[240,8,384]{2,1,0:T(8,128)(2,1)} fusion(bf16[8,240,8,128]{3,1,2,0:T(8,128)(2,1)S(1)} %convolution_convert_fusion, pred[384]{0:T(512)(128)(4,1)S(1)} %compare_and_fusion, pred[128,384]{1,0:T(8,128)(4,1)S(1)} %iota_compare_fusion.6, pred[8,384]{1,0:T(8,128)(4,1)S(1)} %iota_compare_fusion.11), kind=kOutput, calls=%fused_computation.53 | convolution fusion | flops 1511473152 | bytes 5459328 | tf_op jit(solution)/shard_map/rkxn,rnm->kxm/dot_general | solution.py:34
  16.1 2.1 copy.70
  18.2 0.9 fusion.194
  19.1 2.0 copy.126
  21.1 2.9 collective-permute-start
  24.1 2.0 copy.127
  26.1 3.0 collective-permute-start.1
  29.2 2.0 copy.128
  31.2 1.0 copy.129
  32.2 3.8 %collective-permute-start.3 = (bf16[240,8,64]{2,1,0:T(8,128)(2,1)}, bf16[240,8,64]{2,1,0:T(8,128)(2,1)}, u32[]{:S(2)}, u32[]{:S(2)}) collective-permute-start(bf16[240,8,64]{2,1,0:T(8,128)(2,1)} %bitcast.336), channel_id=1, source_target_pairs={{0,6},{1,7},{2,0},{3,1},{4,2},{5,3},{6,4},{7,5},{8,14},{9,15},{10,... | collective-permute-start | bytes 737288 | tf_op jit(solution)/shard_map/ppermute | solution.py:9
  36.0 1.0 copy.130
  37.9 3.3 fusion.66
  42.2 0.9 fusion.71
  45.4 9.1 %fusion.7 = f32[240,8,1024,1]{2,1,3,0:T(8,128)} fusion(bf16[8,240,8,128]{3,1,2,0:T(8,128)(2,1)} %copy-done.1, pred[1024]{0:T(1024)(128)(4,1)S(1)} %get-tuple-element.80, pred[128,1024]{1,0:T(8,128)(4,1)S(1)} %iota_compare_fusion.5, pred[8,1024]{1,0:T(8,128)(4,1)S(1)} %iota_compare_fusion.10), kind=kOutput, calls=%fused_computation.37 | convolution fusion | flops 4028628992 | bytes 11936768 | tf_op jit(solution)/shard_map/rkxn,rnm->kxm/dot_general | solution.py:34
  54.4 7.3 %fusion.5 = f32[240,8,1024,1]{2,1,3,0:T(8,128)} fusion(bf16[8,240,8,128]{3,1,2,0:T(8,128)(2,1)S(1)} %copy-done.2, pred[1024]{0:T(1024)(128)(4,1)S(1)} %get-tuple-element.81, pred[128,1024]{1,0:T(8,128)(4,1)S(1)} %get-tuple-element.106, pred[8,1024]{1,0:T(8,128)(4,1)S(1)} %get-tuple-element.104), kind=kOutput, calls=%fused_computation.35 | convolution fusion | flops 4028628992 | bytes 11936768 | tf_op jit(solution)/shard_map/rkxn,rnm->kxm/dot_general | solution.py:34
  61.8 7.4 %fusion.3 = f32[240,8,1024,1]{2,1,3,0:T(8,128)} fusion(bf16[8,240,8,128]{3,1,2,0:T(8,128)(2,1)S(1)} %copy-done.2, pred[1024]{0:T(1024)(128)(4,1)S(1)} %get-tuple-element.82, pred[128,1024]{1,0:T(8,128)(4,1)S(1)} %get-tuple-element.105, pred[8,1024]{1,0:T(8,128)(4,1)S(1)} %get-tuple-element.103), kind=kOutput, calls=%fused_computation.33 | convolution fusion | flops 4028628992 | bytes 11936768 | tf_op jit(solution)/shard_map/rkxn,rnm->kxm/dot_general | solution.py:34
  69.2 1.0 copy.131
  70.8 33.5 %reduce-scatter.2.cloned.1.call-done = f32[240,8,2]{0,1,2:T(8,128)} async-done(((f32[240,8,16]{0,1,2:T(8,128)}), f32[240,8,2]{0,1,2:T(8,128)}) %reduce-scatter.2.cloned.1.call-update) | async-done | bytes 15376 | tf_op jit(solution)/shard_map/reduce_scatter | solution.py:88
  104.3 67.8 %all_gather.3 = f32[240,8,64]{0,1,2:T(8,128)S(1)} all-gather(f32[240,8,2]{0,1,2:T(8,128)} %reduce-scatter.2.cloned.1.call-done), channel_id=1, replica_groups=mesh['grp'=4,'mem'=8] {'grp','mem'}, dimensions={2}, use_global_device_ids=true | all-gather | bytes 506880 | tf_op jit(solution)/shard_map/all_gather | solution.py:89
  172.1 1.2 convolution_convert_fusion.1
  173.8 0.8 fusion.136
  176.2 4.2 %collective-permute-done.5 = bf16[240,8,64]{2,1,0:T(8,128)(2,1)S(1)} collective-permute-done((bf16[240,8,64]{2,1,0:T(8,128)(2,1)}, bf16[240,8,64]{2,1,0:T(8,128)(2,1)S(1)}, u32[]{:S(2)}, u32[]{:S(2)}) %collective-permute-start.5) | collective-permute-done | bytes 245792 | tf_op jit(solution)/shard_map/ppermute | solution.py:9
  180.5 3.9 %concatenate.23 = bf16[240,8,384]{2,1,0:T(8,128)(2,1)S(1)} concatenate(bf16[240,8,64]{2,1,0:T(8,128)(2,1)} %copy-done.24, bf16[240,8,64]{2,1,0:T(8,128)(2,1)} %copy-done.25, bf16[240,8,64]{2,1,0:T(8,128)(2,1)} %collective-permute-done.2, bf16[240,8,64]{2,1,0:T(8,128)(2,1)} %collective-permute-done.3, bf16[240,8,64]{2,1,0:T(8,128)(2,1)} %collective-permute-done.4, ...), dimensions={2} | concatenate | bytes 2949120 | tf_op jit(solution)/shard_map/concatenate | solution.py:78
  184.3 5.5 %fusion.2 = bf16[240,8,1024]{2,1,0:T(8,128)(2,1)S(1)} fusion(f32[240,8,1024,1]{2,1,3,0:T(8,128)} %fusion.7, bf16[240,8,384]{2,1,0:T(8,128)(2,1)S(1)} %concatenate.23, s32[1024]{0:T(1024)S(1)} %get-tuple-element.70), kind=kOutput, calls=%fused_computation.8 | convolution fusion | flops 1514274816 | bytes 13275136 | tf_op jit(solution)/shard_map/kxa,am->kxm/dot_general | solution.py:111
  189.8 1.4 fusion.191
  191.2 1.5 fusion.44
  192.7 1.5 fusion.46
  194.3 1.6 add_bitcast_fusion.2
  195.9 3.5 %subtract_bitcast_fusion.2 = f32[240,4,1024]{2,0,1:T(8,128)} fusion(f32[4,1024,240]{1,2,0:T(8,128)S(1)} %fusion.46, bf16[240,4,1024]{2,1,0:T(4,128)(2,1)S(1)} %get-tuple-element.38, bf16[3,2,240,240]{3,2,1,0:T(8,128)(2,1)S(1)} %copy-done.21), kind=kOutput, calls=%fused_computation.52 | convolution fusion | flops 472842240 | bytes 9953280 | tf_op jit(solution)/shard_map/kc,cxn->kxn/dot_general | solution.py:18
  199.4 3.3 pad_maximum_fusion
  202.6 5.1 %copy.132 = f32[240,8,8,128]{3,2,1,0:T(8,128)} copy(f32[240,8,8,128]{3,1,2,0:T(8,128)S(1)} %bitcast.330) | data formatting | bytes 15728640
  207.7 5.5 %fusion.1 = bf16[240,8,1024]{2,1,0:T(8,128)(2,1)S(1)} fusion(f32[240,8,1024,1]{2,1,3,0:T(8,128)} %fusion.5, bf16[240,8,384]{2,1,0:T(8,128)(2,1)S(1)} %concatenate.23, s32[1024]{0:T(1024)S(1)} %get-tuple-element.72), kind=kOutput, calls=%fused_computation.6 | convolution fusion | flops 1514274816 | bytes 13275136 | tf_op jit(solution)/shard_map/kxa,am->kxm/dot_general | solution.py:111
  213.2 1.5 fusion.192
  214.8 1.5 fusion.40
  216.3 1.5 fusion.38
  217.8 1.6 subtract_bitcast_fusion.1
  219.4 3.5 %add_bitcast_fusion.1 = f32[240,4,1024]{2,0,1:T(8,128)} fusion(f32[4,1024,240]{1,2,0:T(8,128)S(1)} %fusion.38, bf16[240,4,1024]{2,1,0:T(4,128)(2,1)S(1)} %get-tuple-element.39, bf16[3,2,240,240]{3,2,1,0:T(8,128)(2,1)S(1)} %copy-done.21), kind=kOutput, calls=%fused_computation.49 | convolution fusion | flops 472842240 | bytes 9953280 | tf_op jit(solution)/shard_map/kc,cxn->kxn/dot_general | solution.py:21
  222.9 3.3 pad_maximum_fusion.1
  226.2 5.1 %copy.133 = f32[240,8,8,128]{3,2,1,0:T(8,128)} copy(f32[240,8,8,128]{3,1,2,0:T(8,128)S(1)} %bitcast.331) | data formatting | bytes 15728640
  231.7 1.3 copy.67
  233.0 5.5 %fusion = bf16[240,8,1024]{2,1,0:T(8,128)(2,1)S(1)} fusion(f32[240,8,1024,1]{2,1,3,0:T(8,128)} %fusion.3, bf16[240,8,384]{2,1,0:T(8,128)(2,1)S(1)} %concatenate.23, s32[1024]{0:T(1024)S(1)} %get-tuple-element.75), kind=kOutput, calls=%fused_computation.4 | convolution fusion | flops 1514274816 | bytes 13275136 | tf_op jit(solution)/shard_map/kxa,am->kxm/dot_general | solution.py:111
  238.5 1.6 fusion.193
  240.1 1.5 fusion.34
  241.6 1.5 fusion.32
  243.2 1.6 subtract_bitcast_fusion
  244.8 3.5 %add_bitcast_fusion = f32[240,4,1024]{2,0,1:T(8,128)} fusion(f32[4,1024,240]{1,2,0:T(8,128)S(1)} %fusion.32, bf16[240,4,1024]{2,1,0:T(4,128)(2,1)S(1)} %get-tuple-element.41, bf16[3,2,240,240]{3,2,1,0:T(8,128)(2,1)S(1)} %copy-done.21), kind=kOutput, calls=%fused_computation.47 | convolution fusion | flops 472842240 | bytes 9953280 | tf_op jit(solution)/shard_map/kc,cxn->kxn/dot_general | solution.py:21
  248.3 2.9 pad_maximum_fusion.2
  251.3 5.1 %copy.134 = f32[240,8,8,128]{3,2,1,0:T(8,128)} copy(f32[240,8,8,128]{3,1,2,0:T(8,128)S(1)} %bitcast.332) | data formatting | bytes 15728640
  256.5 22.7 %select_reduce_fusion.2 = (f32[240,8,128]{2,0,1:T(8,128)S(1)}, f32[240,8,128]{2,0,1:T(8,128)S(1)}, f32[240,8,128]{2,0,1:T(8,128)}, f32[240,8,128]{2,0,1:T(8,128)...) fusion(f32[240,8,8,128]{3,2,0,1:T(8,128)S(1)} %bitcast.323, ...), kind=kLoop, calls=%fused_computation.11 | loop fusion | flops 29491200 | bytes 15736832 | tf_op jit(solution)/shard_map/reduce_sum | solution.py:120
  279.3 24.5 %select_reduce_fusion.1 = (f32[240,8,128]{2,0,1:T(8,128)}, f32[240,8,128]{2,0,1:T(8,128)}, f32[240,8,128]{2,0,1:T(8,128)}, f32[240,8,128]{2,0,1:T(8,128)}, f32[2...) fusion(f32[240,8,8,128]{3,2,0,1:T(8,128)S(1)} %bitcast.326, ...), kind=kLoop, calls=%fused_computation.10 | loop fusion | flops 29491200 | bytes 15736832 | tf_op jit(solution)/shard_map/reduce_sum | solution.py:120
  303.9 21.4 %select_reduce_fusion = (f32[240,8,128]{2,0,1:T(8,128)S(1)}, f32[240,8,128]{2,0,1:T(8,128)S(1)}, f32[240,8,128]{2,0,1:T(8,128)S(1)}, f32[240,8,128]{2,0,1:T(8,12...) fusion(f32[240,8,8,128]{3,2,0,1:T(8,128)S(1)} %bitcast.329, ...), kind=kLoop, calls=%fused_computation.9 | loop fusion | flops 29491200 | bytes 15736832 | tf_op jit(solution)/shard_map/reduce_sum | solution.py:120
  325.4 2.6 fusion.96
  328.1 0.9 fusion.98
  329.1 0.9 fusion.100
  330.1 0.9 fusion.102
  331.1 0.9 fusion.104
  332.1 0.9 fusion.106
  333.0 0.9 fusion.108
  334.0 0.9 fusion.110
  334.9 1.2 fusion.63
  336.4 0.9 copy-done.60
  (176 shorter events, 7.8 us)
Async XLA Ops:
  6.5 97.8 %reduce-scatter.2.cloned.1.call-start = ((), (), s32[]{:S(2)}) async-start(), calls=%async_computation.1 | async-start | bytes 147456 | tf_op jit(solution)/shard_map/reduce_scatter | solution.py:88
  18.2 19.0 %copy-start.57 = (s32[128]{0:T(128)S(1)}, s32[128]{0:T(128)}, u32[]{:S(2)}) copy-start(s32[128]{0:T(128)} %param.22) | copy-start | bytes 1540
  21.1 152.2 %collective-permute-start = (bf16[240,8,64]{2,1,0:T(8,128)(2,1)}, bf16[240,8,64]{2,1,0:T(8,128)(2,1)S(1)}, u32[]{:S(2)}, u32[]{:S(2)}) collective-permute-start(bf16[240,8,64]{2,1,0:T(8,128)(2,1)} %bitcast.30), channel_id=1, source_target_pairs={{0,1},{1,2},{2,3},{3,4},{4,5},{5,6},{6,7},{7,0},{8,9},{9,10},{10,1... | collective-permute-start | bytes 737288 | tf_op jit(solution)/shard_map/ppermute | solution.py:9
  24.1 17.2 %copy-start.23 = (bf16[2,240,240]{2,1,0:T(8,128)(2,1)S(1)}, bf16[2,240,240]{2,1,0:T(8,128)(2,1)}, u32[]{:S(2)}) copy-start(bf16[2,240,240]{2,1,0:T(8,128)(2,1)} %param.18) | copy-start | bytes 691204
  26.1 149.3 %collective-permute-start.1 = (bf16[240,8,64]{2,1,0:T(8,128)(2,1)}, bf16[240,8,64]{2,1,0:T(8,128)(2,1)S(1)}, u32[]{:S(2)}, u32[]{:S(2)}) collective-permute-start(bf16[240,8,64]{2,1,0:T(8,128)(2,1)} %bitcast.334), channel_id=1, source_target_pairs={{0,7},{1,0},{2,1},{3,2},{4,3},{5,4},{6,5},{7,6},{8,15},{9,8},{10,9... | collective-permute-start | bytes 737288 | tf_op jit(solution)/shard_map/ppermute | solution.py:9
  31.2 144.3 %collective-permute-start.2 = (bf16[240,8,64]{2,1,0:T(8,128)(2,1)}, bf16[240,8,64]{2,1,0:T(8,128)(2,1)}, u32[]{:S(2)}, u32[]{:S(2)}) collective-permute-start(bf16[240,8,64]{2,1,0:T(8,128)(2,1)} %bitcast.335), channel_id=1, source_target_pairs={{0,2},{1,3},{2,4},{3,5},{4,6},{5,7},{6,0},{7,1},{8,10},{9,11},{10,... | collective-permute-start | bytes 737288 | tf_op jit(solution)/shard_map/ppermute | solution.py:9
  32.2 143.2 %collective-permute-start.3 = (bf16[240,8,64]{2,1,0:T(8,128)(2,1)}, bf16[240,8,64]{2,1,0:T(8,128)(2,1)}, u32[]{:S(2)}, u32[]{:S(2)}) collective-permute-start(bf16[240,8,64]{2,1,0:T(8,128)(2,1)} %bitcast.336), channel_id=1, source_target_pairs={{0,6},{1,7},{2,0},{3,1},{4,2},{5,3},{6,4},{7,5},{8,14},{9,15},{10,... | collective-permute-start | bytes 737288 | tf_op jit(solution)/shard_map/ppermute | solution.py:9
  37.0 138.4 %collective-permute-start.4 = (bf16[240,8,64]{2,1,0:T(8,128)(2,1)}, bf16[240,8,64]{2,1,0:T(8,128)(2,1)}, u32[]{:S(2)}, u32[]{:S(2)}) collective-permute-start(bf16[240,8,64]{2,1,0:T(8,128)(2,1)} %bitcast.337), channel_id=1, source_target_pairs={{0,8},{8,16},{16,24},{24,0},{1,9},{9,17},{17,25},{25,1},{2,10},{10... | collective-permute-start | bytes 737288 | tf_op jit(solution)/shard_map/ppermute | solution.py:9
  37.9 4.3 %copy-start.46 = (s32[128]{0:T(128)S(1)}, s32[128]{0:T(128)}, u32[]{:S(2)}) copy-start(s32[128]{0:T(128)} %param.21) | copy-start | bytes 1540
  41.3 2.6 copy-start.28
  41.3 2.8 copy-start.29
  41.3 3.3 copy-start.56
  45.4 9.1 %copy-start.2 = (bf16[8,240,8,128]{3,1,2,0:T(8,128)(2,1)S(1)}, bf16[8,240,8,128]{3,1,2,0:T(8,128)(2,1)}, u32[]{:S(2)}) copy-start(bf16[8,240,8,128]{3,1,2,0:T(8,128)(2,1)} %copy-done.1) | copy-start | bytes 11796484
  61.8 112.0 %copy-start.22 = (bf16[2,240,240]{2,1,0:T(8,128)(2,1)S(1)}, bf16[2,240,240]{2,1,0:T(8,128)(2,1)}, u32[]{:S(2)}) copy-start(bf16[2,240,240]{2,1,0:T(8,128)(2,1)} %param.19) | copy-start | bytes 691204
  173.3 2.1 copy-start.24
  173.3 7.1 %collective-permute-start.5 = (bf16[240,8,64]{2,1,0:T(8,128)(2,1)}, bf16[240,8,64]{2,1,0:T(8,128)(2,1)S(1)}, u32[]{:S(2)}, u32[]{:S(2)}) collective-permute-start(bf16[240,8,64]{2,1,0:T(8,128)(2,1)} %bitcast.338), channel_id=1, source_target_pairs={{0,24},{8,0},{16,8},{24,16},{1,25},{9,1},{17,9},{25,17},{2,26},{10... | collective-permute-start | bytes 737288 | tf_op jit(solution)/shard_map/ppermute | solution.py:9
  226.2 5.1 %copy-start.27 = (f32[4,16,240]{2,1,0:T(8,128)S(1)}, f32[4,16,240]{2,1,0:T(8,128)}, u32[]{:S(2)}) copy-start(f32[4,16,240]{2,1,0:T(8,128)} %fusion.136) | copy-start | bytes 184324
  226.2 5.3 %copy-start.26 = (f32[4,16,240]{2,1,0:T(8,128)S(1)}, f32[4,16,240]{2,1,0:T(8,128)}, u32[]{:S(2)}) copy-start(f32[4,16,240]{2,1,0:T(8,128)} %fusion.138) | copy-start | bytes 184324
  251.2 5.2 %slice-start = ((s8[7864320]{0:T(1024)(128)(4,1)}), s8[4194304]{0:T(1024)(128)(4,1)S(1)}, s32[]{:S(2)}) async-start(s8[7864320]{0:T(1024)(128)(4,1)} %bitcast.321), calls=%async_computation.2 | async-start | bytes 8388608
  251.2 5.2 %slice-start.1 = ((s8[7864320]{0:T(1024)(128)(4,1)}), s8[3670016]{0:T(1024)(128)(4,1)S(1)}, s32[]{:S(2)}) async-start(s8[7864320]{0:T(1024)(128)(4,1)} %bitcast.321), calls=%async_computation.3 | async-start | bytes 7340032
  251.2 5.2 %copy-start.31 = (pred[8,128]{1,0:T(8,128)(4,1)S(1)}, pred[8,128]{1,0:T(8,128)(4,1)}, u32[]{:S(2)}) copy-start(pred[8,128]{1,0:T(8,128)(4,1)} %get-tuple-element.51) | copy-start | bytes 3076
  251.2 5.2 %copy-start.32 = (pred[8,128]{1,0:T(8,128)(4,1)S(1)}, pred[8,128]{1,0:T(8,128)(4,1)}, u32[]{:S(2)}) copy-start(pred[8,128]{1,0:T(8,128)(4,1)} %get-tuple-element.52) | copy-start | bytes 3076
  251.2 5.2 %copy-start.33 = (pred[8,128]{1,0:T(8,128)(4,1)S(1)}, pred[8,128]{1,0:T(8,128)(4,1)}, u32[]{:S(2)}) copy-start(pred[8,128]{1,0:T(8,128)(4,1)} %get-tuple-element.53) | copy-start | bytes 3076
  251.2 5.2 %copy-start.34 = (pred[8,128]{1,0:T(8,128)(4,1)S(1)}, pred[8,128]{1,0:T(8,128)(4,1)}, u32[]{:S(2)}) copy-start(pred[8,128]{1,0:T(8,128)(4,1)} %get-tuple-element.54) | copy-start | bytes 3076
  251.3 5.2 %copy-start.35 = (pred[8,128]{1,0:T(8,128)(4,1)S(1)}, pred[8,128]{1,0:T(8,128)(4,1)}, u32[]{:S(2)}) copy-start(pred[8,128]{1,0:T(8,128)(4,1)} %get-tuple-element.55) | copy-start | bytes 3076
  251.3 5.2 %copy-start.36 = (pred[8,128]{1,0:T(8,128)(4,1)S(1)}, pred[8,128]{1,0:T(8,128)(4,1)}, u32[]{:S(2)}) copy-start(pred[8,128]{1,0:T(8,128)(4,1)} %get-tuple-element.56) | copy-start | bytes 3076
  251.3 5.2 %copy-start.37 = (pred[8,128]{1,0:T(8,128)(4,1)S(1)}, pred[8,128]{1,0:T(8,128)(4,1)}, u32[]{:S(2)}) copy-start(pred[8,128]{1,0:T(8,128)(4,1)} %get-tuple-element.57) | copy-start | bytes 3076
  251.3 5.2 %copy-start.38 = (pred[8,128]{1,0:T(8,128)(4,1)S(1)}, pred[8,128]{1,0:T(8,128)(4,1)}, u32[]{:S(2)}) copy-start(pred[8,128]{1,0:T(8,128)(4,1)} %get-tuple-element.58) | copy-start | bytes 3076
  256.4 22.8 %slice-start.2 = ((s8[7864320]{0:T(1024)(128)(4,1)}), s8[4194304]{0:T(1024)(128)(4,1)S(1)}, s32[]{:S(2)}) async-start(s8[7864320]{0:T(1024)(128)(4,1)} %bitcast.324), calls=%async_computation.4 | async-start | bytes 8388608
  256.5 22.7 %slice-start.3 = ((s8[7864320]{0:T(1024)(128)(4,1)}), s8[3670016]{0:T(1024)(128)(4,1)S(1)}, s32[]{:S(2)}) async-start(s8[7864320]{0:T(1024)(128)(4,1)} %bitcast.324), calls=%async_computation.5 | async-start | bytes 7340032
  256.5 22.7 %copy-start.30 = (pred[8,128]{1,0:T(8,128)(4,1)S(1)}, pred[8,128]{1,0:T(8,128)(4,1)}, u32[]{:S(2)}) copy-start(pred[8,128]{1,0:T(8,128)(4,1)} %get-tuple-element.65) | copy-start | bytes 3076
  256.5 22.7 %copy-start.45 = (pred[8,128]{1,0:T(8,128)(4,1)S(1)}, pred[8,128]{1,0:T(8,128)(4,1)}, u32[]{:S(2)}) copy-start(pred[8,128]{1,0:T(8,128)(4,1)} %get-tuple-element.83) | copy-start | bytes 3076
  279.2 24.6 %slice-start.4 = ((s8[7864320]{0:T(1024)(128)(4,1)}), s8[4194304]{0:T(1024)(128)(4,1)S(1)}, s32[]{:S(2)}) async-start(s8[7864320]{0:T(1024)(128)(4,1)} %bitcast.327), calls=%async_computation.6 | async-start | bytes 8388608
  279.2 24.6 %slice-start.5 = ((s8[7864320]{0:T(1024)(128)(4,1)}), s8[3670016]{0:T(1024)(128)(4,1)S(1)}, s32[]{:S(2)}) async-start(s8[7864320]{0:T(1024)(128)(4,1)} %bitcast.327), calls=%async_computation.7 | async-start | bytes 7340032
  279.3 24.6 %copy-start.41 = (pred[8,128]{1,0:T(8,128)(4,1)S(1)}, pred[8,128]{1,0:T(8,128)(4,1)}, u32[]{:S(2)}) copy-start(pred[8,128]{1,0:T(8,128)(4,1)} %get-tuple-element.84) | copy-start | bytes 3076
  279.3 24.6 %copy-start.42 = (pred[8,128]{1,0:T(8,128)(4,1)S(1)}, pred[8,128]{1,0:T(8,128)(4,1)}, u32[]{:S(2)}) copy-start(pred[8,128]{1,0:T(8,128)(4,1)} %get-tuple-element.85) | copy-start | bytes 3076
  279.3 24.6 %copy-start.43 = (pred[8,128]{1,0:T(8,128)(4,1)S(1)}, pred[8,128]{1,0:T(8,128)(4,1)}, u32[]{:S(2)}) copy-start(pred[8,128]{1,0:T(8,128)(4,1)} %get-tuple-element.86) | copy-start | bytes 3076
  279.3 24.6 %copy-start.44 = (pred[8,128]{1,0:T(8,128)(4,1)S(1)}, pred[8,128]{1,0:T(8,128)(4,1)}, u32[]{:S(2)}) copy-start(pred[8,128]{1,0:T(8,128)(4,1)} %get-tuple-element.87) | copy-start | bytes 3076
  303.9 21.4 %copy-start.4 = (f32[240,8,16]{2,1,0:T(8,128)S(1)}, f32[240,8,16]{2,1,0:T(8,128)}, u32[]{:S(2)}) copy-start(f32[240,8,16]{2,1,0:T(8,128)} %copy.67) | copy-start | bytes 368644
  303.9 21.4 %copy-start.13 = (f32[240,8,128]{2,0,1:T(8,128)S(1)}, f32[240,8,128]{2,0,1:T(8,128)}, u32[]{:S(2)}) copy-start(f32[240,8,128]{2,0,1:T(8,128)} %get-tuple-element.12) | copy-start | bytes 2949124
  303.9 21.4 %copy-start.17 = (f32[240,8,128]{2,0,1:T(8,128)S(1)}, f32[240,8,128]{2,0,1:T(8,128)}, u32[]{:S(2)}) copy-start(f32[240,8,128]{2,0,1:T(8,128)} %get-tuple-element.20) | copy-start | bytes 2949124
  303.9 21.4 %copy-start.47 = (s32[128]{0:T(128)S(1)}, s32[128]{0:T(128)}, u32[]{:S(2)}) copy-start(s32[128]{0:T(128)} %param.21) | copy-start | bytes 1540
  303.9 21.4 %copy-start.55 = (pred[128]{0:T(512)(128)(4,1)S(1)}, pred[128]{0:T(512)(128)(4,1)}, u32[]{:S(2)}) copy-start(pred[128]{0:T(512)(128)(4,1)} %get-tuple-element.99) | copy-start | bytes 388
  325.3 2.8 copy-start.11
  325.3 2.8 copy-start.16
  325.3 2.8 copy-start.20
  325.3 2.8 copy-start.54
  325.4 3.7 %copy-start.9 = (f32[240,8,128]{2,0,1:T(8,128)S(1)}, f32[240,8,128]{2,0,1:T(8,128)}, u32[]{:S(2)}) copy-start(f32[240,8,128]{2,0,1:T(8,128)} %get-tuple-element.10) | copy-start | bytes 2949124
  325.4 3.7 %copy-start.15 = (f32[240,8,128]{2,0,1:T(8,128)S(1)}, f32[240,8,128]{2,0,1:T(8,128)}, u32[]{:S(2)}) copy-start(f32[240,8,128]{2,0,1:T(8,128)} %get-tuple-element.18) | copy-start | bytes 2949124
  325.4 3.7 %copy-start.19 = (f32[240,8,128]{2,0,1:T(8,128)S(1)}, f32[240,8,128]{2,0,1:T(8,128)}, u32[]{:S(2)}) copy-start(f32[240,8,128]{2,0,1:T(8,128)} %get-tuple-element.26) | copy-start | bytes 2949124
  325.4 3.7 %copy-start.53 = (pred[128]{0:T(512)(128)(4,1)S(1)}, pred[128]{0:T(512)(128)(4,1)}, u32[]{:S(2)}) copy-start(pred[128]{0:T(512)(128)(4,1)} %get-tuple-element.96) | copy-start | bytes 388
  328.1 2.0 copy-start.7
  328.1 2.0 copy-start.14
  328.1 2.0 copy-start.18
  328.1 2.0 copy-start.52
  329.1 1.9 copy-start.6
  329.1 1.9 copy-start.12
  329.1 1.9 copy-start.51
  330.1 1.9 copy-start.3
  330.1 1.9 copy-start.10
  330.1 1.9 copy-start.50
  331.1 1.9 copy-start.8
  331.1 1.9 copy-start.49
  332.0 1.9 copy-start.5
  (10 other events, 13.8 us)
Sparse Core Ops, SparseCore 0:
  44.0 60.2 reduce-scatter.1
where the time goes:
time: 350 us; the launch traced here: 344 us
  other arithmetic  86.8 us (25%)
  matrix products  83.2 us (24%)
  blocking collectives  67.8 us (19%)
  local copies, waits for them, and re-layouts  43.5 us (12%)
  waiting for transfers between devices  37.8 us (11%)
  between operations  14.8 us (4%)
  starting transfers between devices  10.4 us (3%)
    reduce_sum x3, other arithmetic, on_device(): partial_rot[rot_idx] = partial_rot[rot_idx] + jnp.sum(chosen, axis=2)  68.6 us
    all_gather x1, blocking collectives, on_device(): expansions = lax.all_gather(shares, ('grp', 'mem'), axis=2, tiled=True)  67.8 us
    reduce_scatter x1, waiting for transfers between devices, on_device(): lax.psum_scatter(partial_exp, 'mem', scatter_dimension=2, tiled=True)  33.5 us
    dot_general x5, matrix products, pool_select(): jnp.einsum('rkxn,rnm->kxm', rotated, selector, preferred_element_type=jnp...  31.1 us
    unnamed x143, local copies, waits for them, and re-layouts  28.6 us
    dot_general x3, matrix products, on_device(): jnp.einsum('kxa,am->kxm', arrived, recv_select, preferred_element_type=jn...  16.4 us
    ppermute x6, starting transfers between devices, shifted(): lax.ppermute(value, axis, [(i, (i + by) % length) for i in range(length)])  10.4 us
    concatenate x4, other arithmetic, complex_apply(): return jnp.concatenate([real_out, imag_out], axis=1)  9.47 us
  transfers between devices with their start and end apart: 7, of which 2 were waited for; matrix products, arithmetic and copies ran while one was open for 12% of the time, Pallas kernels for 0%

commit v1 on v0

v1 whole, which is shorter than its diff:
```python
import functools

import jax
import jax.numpy as jnp
from jax import lax
from jax.experimental import pallas as pl
from jax.experimental.pallas import tpu as pltpu
from jax.sharding import PartitionSpec as P

F32 = jnp.float32
BF16 = jnp.bfloat16
MIB = 1 << 20


def shifted(value, axis, by):
    length = lax.axis_size(axis)
    return lax.ppermute(value, axis, [(i, (i + by) % length) for i in range(length)])


def dot_nn(a, b):
    return jnp.dot(a, b, preferred_element_type=F32)


def dot_nt(a, b):
    return lax.dot_general(a, b, (((1,), (1,)), ((), ())), preferred_element_type=F32)


def rotate_kernel(peers, width, coef_ref, rot_ref, send_ref, clus_ref, crot_ref, *rest):
    pool_ref, sums_ref = rest[0], rest[1]
    out_refs = rest[2 : 2 + peers]
    sel = rest[2 + peers]
    comps, n_coef, sph = coef_ref.shape
    rots = rot_ref.shape[0]
    pool = rots * sph
    group = sums_ref.shape[0]
    x_all = jnp.concatenate([coef_ref[x].astype(BF16) for x in range(comps)], axis=1)
    for r in range(rots):
        turned = dot_nn(rot_ref[r], x_all).astype(BF16)
        for x in range(comps):
            pool_ref[x * n_coef : (x + 1) * n_coef, r * sph : (r + 1) * sph] = turned[
                :, x * sph : (x + 1) * sph
            ]
    total = peers * width
    col_iota = lax.broadcasted_iota(jnp.int32, (total, sph), 1)
    clus_iota = lax.broadcasted_iota(jnp.int32, (group, sph), 0)
    for r in range(rots):
        hit = send_ref[...] == col_iota + r * sph
        sel[:total, r * sph : (r + 1) * sph] = jnp.where(hit, 1.0, 0.0).astype(BF16)
        own = (clus_ref[...] == clus_iota) & (crot_ref[...] == r)
        sel[total:, r * sph : (r + 1) * sph] = jnp.where(own, 1.0, 0.0).astype(BF16)
    rows = comps * n_coef
    step = 3 * sph
    for at in range(0, rows, step):
        picked = dot_nt(sel[...], pool_ref[at : at + step, :])
        for p in range(peers):
            out_refs[p][:, at : at + step] = picked[p * width : (p + 1) * width].astype(BF16)
        sums_ref[:, at : at + step] = picked[total:]


def gather_kernel(
    peers,
    per_shell,
    pool_ref,
    exp_ref,
    *rest,
):
    recv_refs = rest[:peers]
    (
        coup_ref, axial_ref, up_ref, far_ref, rott_ref, mie_ref, inc_ref,
        gid_ref, crot_ref, pcol_ref, prot_ref, out_ref,
        recv_s, count_s, sel_s, taken_s, far_s, gath_s,
    ) = rest[peers:]
    comps, n_coef, sph = inc_ref.shape
    dirs = comps // 2
    slots = pcol_ref.shape[0]
    shells = slots // per_shell
    pool = pool_ref.shape[1]
    rots = pool // sph
    width = recv_refs[0].shape[0]
    total = peers * width
    clus = coup_ref.shape[0]
    half = dirs * sph

    arrived = jnp.concatenate([recv_refs[p][...] for p in range(peers)], axis=0)
    recv_s[...] = arrived.T

    q_iota = lax.broadcasted_iota(jnp.int32, (total, sph), 0) + pool
    rot_of = jnp.full((total, sph), -1.0, F32)
    for h in range(shells):
        count = jnp.zeros((total, sph), F32)
        for s in range(h * per_shell, (h + 1) * per_shell):
            hit = pcol_ref[s : s + 1, :] == q_iota
            count = count + jnp.where(hit, 1.0, 0.0)
            rot_of = jnp.where(hit, prot_ref[s : s + 1, :].astype(F32), rot_of)
        count_s[:, h * sph : (h + 1) * sph] = count.astype(BF16)
    rot_of = jnp.max(rot_of, axis=1, keepdims=True)

    clus_iota = lax.broadcasted_iota(jnp.int32, (clus, sph), 0)
    member = jnp.where(gid_ref[...] == clus_iota, 1.0, 0.0).astype(F32)
    weights = jnp.dot(coup_ref[...], member, precision=lax.Precision.HIGHEST, preferred_element_type=F32)
    near_sum = jnp.dot(
        exp_ref[...].T, weights, precision=lax.Precision.HIGHEST, preferred_element_type=F32
    )
    folded = jnp.concatenate(
        [
            jnp.concatenate(
                [near_sum[(c * dirs + d) * n_coef : (c * dirs + d + 1) * n_coef] for d in range(dirs)],
                axis=1,
            )
            for c in range(2)
        ],
        axis=0,
    )
    high = folded.astype(BF16)
    low = (folded - high.astype(F32)).astype(BF16)
    reached = dot_nn(up_ref[...], high) + dot_nn(up_ref[...], low)
    far_s[...] = dot_nn(far_ref[...], reached.astype(BF16))

    j_iota = lax.broadcasted_iota(jnp.int32, (sph, sph), 0)

    @pl.loop(0, rots)
    def _(r):
        first = pl.multiple_of(r * sph, sph)
        ids = j_iota + r * sph
        for h in range(shells):
            count = jnp.zeros((sph, sph), F32)
            for s in range(h * per_shell, (h + 1) * per_shell):
                count = count + jnp.where(pcol_ref[s : s + 1, :] == ids, 1.0, 0.0)
            sel_s[:sph, h * sph : (h + 1) * sph] = count.astype(BF16)
        mine = rot_of == r.astype(F32)
        sel_s[sph:, :] = jnp.where(mine, count_s[...].astype(F32), 0.0).astype(BF16)
        sel = sel_s[...]
        for x in range(comps):
            c, d = x // dirs, x % dirs
            rows = slice(x * n_coef, (x + 1) * n_coef)
            lhs = jnp.concatenate([pool_ref[rows, pl.ds(first, sph)], recv_s[rows, :]], axis=1)
            taken = dot_nn(lhs, sel).astype(BF16)
            for h in range(shells):
                at = (h * 2 + c) * n_coef
                taken_s[at : at + n_coef, d * sph : (d + 1) * sph] = taken[:, h * sph : (h + 1) * sph]
        moved = dot_nn(axial_ref[...], taken_s[...])
        here = jnp.concatenate([crot_ref[...]] * dirs, axis=1) == r
        summed = (moved + jnp.where(here, far_s[...], 0.0)).astype(BF16)
        gath_s[r, :, :half] = summed[:n_coef]
        gath_s[r, :, half:] = summed[n_coef:]

    field = dot_nn(rott_ref[...], gath_s[...].reshape(rots * n_coef, comps * sph))
    mie_r = mie_ref[:, 0:1]
    mie_i = mie_ref[:, 1:2]
    for d in range(dirs):
        re = inc_ref[d] + field[:, d * sph : (d + 1) * sph]
        im = inc_ref[dirs + d] + field[:, half + d * sph : half + (d + 1) * sph]
        out_ref[d] = mie_r * re - mie_i * im
        out_ref[dirs + d] = mie_r * im + mie_i * re


def complex_block(pair):
    return jnp.concatenate(
        [
            jnp.concatenate([pair[..., 0, :, :], -pair[..., 1, :, :]], axis=-1),
            jnp.concatenate([pair[..., 1, :, :], pair[..., 0, :, :]], axis=-1),
        ],
        axis=-2,
    )


def on_device(
    coefficients,
    incident,
    mie_coeffs,
    rot_table,
    axial_shells,
    up_axial,
    far_axial,
    coupling,
    cluster_ids,
    center_rot,
    pair_col,
    pair_rot,
    send_col,
):
    comps, n_coef, sph = coefficients.shape
    rots = rot_table.shape[0]
    pool = rots * sph
    rows = comps * n_coef
    clus = coupling.shape[0]
    group = clus // lax.axis_size("grp")
    peers, width = send_col.shape
    total = peers * width
    shells = axial_shells.shape[0]
    per_shell = pair_col.shape[0] // shells
    dirs = comps // 2
    vmem = pl.BlockSpec(memory_space=pltpu.VMEM)
    clus_row = cluster_ids.reshape(1, sph)
    crot_row = center_rot.reshape(1, sph)

    first = pl.pallas_call(
        functools.partial(rotate_kernel, peers, width),
        out_shape=[
            jax.ShapeDtypeStruct((rows, pool), BF16),
            jax.ShapeDtypeStruct((group, rows), F32),
        ]
        + [jax.ShapeDtypeStruct((width, rows), BF16)] * peers,
        in_specs=[vmem] * 5,
        out_specs=[vmem] * (2 + peers),
        scratch_shapes=[pltpu.VMEM((total + group, pool), BF16)],
        compiler_params=pltpu.CompilerParams(vmem_limit_bytes=40 * MIB),
        name="rotate",
    )(coefficients, rot_table, send_col.reshape(total, 1), clus_row, crot_row)
    rotated, sums = first[0], first[1]
    outgoing = first[2:]
    shares = lax.psum_scatter(sums, "mem", scatter_dimension=0, tiled=True)
    expansions = lax.all_gather(shares, ("grp", "mem"), axis=0, tiled=True)
    mem_moves = [1, -1, 2, -2]
    grp_moves = [1, -1]
    received = [shifted(outgoing[i], "mem", by) for i, by in enumerate(mem_moves)]
    received += [
        shifted(outgoing[len(mem_moves) + i], "grp", by) for i, by in enumerate(grp_moves)
    ]

    axial = complex_block(axial_shells)
    axial = jnp.transpose(axial, (1, 0, 2)).reshape(2 * n_coef, shells * 2 * n_coef)
    up = complex_block(up_axial)
    far = complex_block(far_axial)
    rott = jnp.transpose(rot_table, (2, 0, 1)).reshape(n_coef, rots * n_coef)
    eye = jnp.arange(clus)[:, None] == jnp.arange(clus)[None, :]
    coup_t = jnp.where(eye, F32(0.0), coupling).T
    gid = clus_row + lax.axis_index("grp") * group
    half = dirs * sph
    return pl.pallas_call(
        functools.partial(gather_kernel, peers, per_shell),
        out_shape=jax.ShapeDtypeStruct((comps, n_coef, sph), F32),
        in_specs=[vmem] * (13 + peers),
        out_specs=vmem,
        scratch_shapes=[
            pltpu.VMEM((rows, total), BF16),
            pltpu.VMEM((total, shells * sph), BF16),
            pltpu.VMEM((sph + total, shells * sph), BF16),
            pltpu.VMEM((shells * 2 * n_coef, half), BF16),
            pltpu.VMEM((2 * n_coef, half), F32),
            pltpu.VMEM((rots, n_coef, comps * sph), BF16),
        ],
        compiler_params=pltpu.CompilerParams(vmem_limit_bytes=48 * MIB),
        name="gather",
    )(
        rotated, expansions, *received, coup_t, axial, up, far, rott, mie_coeffs.T, incident,
        gid, crot_row, pair_col, pair_rot,
    )


def solution(mesh):
    cut = ("grp", "mem")
    in_specs = (
        P(None, None, cut),
        P(None, None, cut),
        P(),
        P(),
        P(),
        P(),
        P(),
        P(),
        P(cut),
        P(cut),
        P(None, cut),
        P(None, cut),
        P(cut, None),
    )
    return jax.shard_map(
        on_device, mesh=mesh, in_specs=in_specs, out_specs=P(None, None, cut), check_vma=False
    )
```

time: 350 us -> 204 us (0.58); the launches traced: 344 us -> 204 us
  matrix products: 83.2 us -> 0 us
  other arithmetic: 86.8 us -> 5.15 us
  Pallas kernels: 0 us -> 31.4 us
  local copies, waits for them, and re-layouts: 43.5 us -> 17 us
  waiting for transfers between devices: 37.8 us -> 51.6 us
  blocking collectives: 67.8 us -> 72.5 us
    dot_general x33 -> x0, matrix products: 83.2 us -> none  [the longest x5 31.1 us: pool_select(): jnp.einsum('rkxn,rnm->kxm', rotated, selector, preferred_element_type=jnp...]
    reduce_sum x3 -> x0, other arithmetic: 68.6 us -> none  [on_device(): partial_rot[rot_idx] = partial_rot[rot_idx] + jnp.sum(chosen, axis=2)]
    unnamed x1 -> x2, waiting for transfers between devices: 0.02 us -> 51.5 us
    reduce_scatter x1 -> x0, waiting for transfers between devices: 33.5 us -> none  [on_device(): lax.psum_scatter(partial_exp, 'mem', scatter_dimension=2, tiled=True)]
    pallas_call x0 -> x2, Pallas kernels: none -> 31.4 us  [the longest x1 26.8 us: on_device(): pl.pallas_call(functools.partial(gather_kernel, peers, per_shell), out_sh...]
    unnamed x143 -> x37, local copies, waits for them, and re-layouts: 28.6 us -> 11 us
    concatenate x4 -> x2, other arithmetic: 9.47 us -> 3.45 us  [complex_block(): jnp.concatenate([jnp.concatenate([pair[..., 0, :, :], -pair[..., 1, :, :]...]
    slice x5 -> x1, local copies, waits for them, and re-layouts: 6 us -> 0.05 us  [complex_block(): pair[..., 1, :, :]]
  transfers between devices with their start and end apart: 7 -> 7, of which waited for: 2 -> 1; matrix products, arithmetic and copies ran while one was open for 12% -> 7% of each run, Pallas kernels for 0% -> 0%
where the time goes in v1:
time: 204 us
  blocking collectives  72.5 us (36%)
  waiting for transfers between devices  51.6 us (25%)
  Pallas kernels  31.4 us (15%)
  local copies, waits for them, and re-layouts  17 us (8%)
  between operations  14.2 us (7%)
  starting transfers between devices  11.7 us (6%)
  other arithmetic  5.15 us (3%)
    all_gather x1, blocking collectives, on_device(): expansions = lax.all_gather(shares, ('grp', 'mem'), axis=0, tiled=True)  72.5 us
    unnamed x2, waiting for transfers between devices  51.5 us
    pallas_call x1, Pallas kernels, on_device(): pl.pallas_call(functools.partial(gather_kernel, peers, per_shell), out_sh...  26.8 us
    ppermute x6, starting transfers between devices, shifted(): lax.ppermute(value, axis, [(i, (i + by) % length) for i in range(length)])  11.7 us
    unnamed x37, local copies, waits for them, and re-layouts  11 us
    pallas_call x1, Pallas kernels, on_device(): pl.pallas_call(functools.partial(rotate_kernel, peers, width), out_shape=...  4.63 us
  transfers between devices with their start and end apart: 7, of which 1 were waited for; matrix products, arithmetic and copies ran while one was open for 7% of the time, Pallas kernels for 0%

profile of v1, /device:TPU:0, one launch (start us, length us, event | category | flops | bytes accessed | tf_op | source)
XLA Modules:
  0.0 203.6 jit_solution(15406957669759569664)
XLA Ops:
  6.5 0.0 copy-start.10
  6.5 0.0 copy-start.13
  6.5 0.0 copy-start.14
  6.5 0.0 all-reduce.3.cloned.1.call-start
  6.5 0.9 reshape.24.send_ref
  7.4 0.0 copy-start
  7.4 1.2 copy-done
  8.6 0.0 copy-start.3
  8.6 1.2 copy-done.3
  9.8 0.0 copy-start.7
  9.8 0.7 copy-done.7
  10.5 0.0 copy-start.9
  10.5 0.7 copy-done.9
  11.2 0.0 copy-start.12
  11.2 0.0 copy-start.11
  11.2 4.6 %rotate.1 = (bf16[1920,1024]{1,0:T(8,128)(2,1)S(1)}, f32[16,1920]{1,0:T(8,128)}, bf16[64,1920]{1,0:T(8,128)(2,1)S(1)}, bf16[64,1920]{1,0:T(8,128)(2,1)}, bf16[64...) custom-call(f32[8,240,128]{2,1,0:T(8,128)S(1)} %copy-done.3, ...), custom_call_target="tpu_custom_call" | custom-call | tf_op jit(solution)/shard_map/rotate/pallas_call | solution.py:197
  15.8 0.0 copy-start.2
  15.8 1.9 copy-done.2
  17.7 0.0 all-reduce.3.cloned.1.call-update
  17.7 3.0 %collective-permute-start = (bf16[64,1920]{1,0:T(8,128)(2,1)S(1)}, bf16[64,1920]{1,0:T(8,128)(2,1)}, u32[]{:S(2)}, u32[]{:S(2)}) collective-permute-start(bf16[64,1920]{1,0:T(8,128)(2,1)S(1)} %get-tuple-element.15), channel_id=1, source_target_pairs={{0,1},{1,2},{2,3},{3,4},{4,5},{5,6},{6,7},{7,0},{8,9},{9,10},{10,1... | collective-permute-start | bytes 737288 | tf_op jit(solution)/shard_map/ppermute | solution.py:17
  20.7 3.1 %collective-permute-start.1 = (bf16[64,1920]{1,0:T(8,128)(2,1)}, bf16[64,1920]{1,0:T(8,128)(2,1)}, u32[]{:S(2)}, u32[]{:S(2)}) collective-permute-start(bf16[64,1920]{1,0:T(8,128)(2,1)} %get-tuple-element.16), channel_id=1, source_target_pairs={{0,7},{1,0},{2,1},{3,2},{4,3},{5,4},{6,5},{7,6},{8,15},{9,8},{10,9... | collective-permute-start | bytes 737288 | tf_op jit(solution)/shard_map/ppermute | solution.py:17
  23.8 0.0 collective-permute-start.2
  23.8 3.8 %collective-permute-start.3 = (bf16[64,1920]{1,0:T(8,128)(2,1)}, bf16[64,1920]{1,0:T(8,128)(2,1)}, u32[]{:S(2)}, u32[]{:S(2)}) collective-permute-start(bf16[64,1920]{1,0:T(8,128)(2,1)} %get-tuple-element.18), channel_id=1, source_target_pairs={{0,6},{1,7},{2,0},{3,1},{4,2},{5,3},{6,4},{7,5},{8,14},{9,15},{10,... | collective-permute-start | bytes 737288 | tf_op jit(solution)/shard_map/ppermute | solution.py:17
  27.6 0.0 collective-permute-start.4
  27.6 0.9 fusion
  28.5 1.7 slice_bitcast_fusion.2
  30.2 0.0 copy-done.12
  30.2 0.7 slice_bitcast_fusion
  31.0 0.0 copy-done.10
  31.0 0.0 copy-done.13
  31.0 0.1 copy.27
  31.1 0.0 copy-done.14
  31.1 0.1 copy.31
  31.2 0.0 copy-done.11
  31.2 0.1 fusion.2
  31.3 0.2 copy.35
  31.5 0.8 bitcast_negate_fusion
  32.2 0.9 copy.34
  33.1 0.0 copy-start.1
  33.2 1.9 maximum_maximum_fusion
  35.0 1.7 copy.32.rest_7_
  36.8 0.0 copy-start.4
  36.8 0.0 copy-start.5
  36.8 0.0 copy-done.1
  36.8 0.8 copy.33.rest_10_
  37.6 1.2 dynamic-slice
  39.5 1.6 maximum_maximum_fusion.1
  41.1 0.0 collective-permute-done.rest_0_
  41.1 1.8 collective-permute-start.5
  42.9 51.5 %all-reduce.3.cloned.1.call-done = f32[16,1920]{1,0:T(8,128)} async-done(((f32[16,1920]{1,0:T(8,128)}), f32[16,1920]{1,0:T(8,128)}) %all-reduce.3.cloned.1.call-update) | async-done | bytes 122896
  94.5 0.8 dynamic-slice_bitcast_fusion
  95.3 72.5 %all-gather = f32[32,2,1920]{2,1,0:T(2,128)} all-gather(f32[1,2,1920]{2,1,0:T(2,128)S(1)} %dynamic-slice_bitcast_fusion), channel_id=1, replica_groups=mesh['grp'=4,'mem'=8] {'grp','mem'}, dimensions={0}, use_global_device_ids=true | all-gather | bytes 506880 | tf_op jit(solution)/shard_map/all_gather | solution.py:213
  167.8 1.4 reshape.22.exp_ref
  169.2 0.0 collective-permute-done.1.rest_1_
  169.2 0.0 collective-permute-done.2.rest_2_
  169.2 0.0 collective-permute-done.3.rest_3_
  169.2 0.0 collective-permute-done.4.rest_4_
  169.3 0.0 collective-permute-done.5.rest_5_
  169.3 0.0 copy-done.4
  169.3 0.0 copy-done.5
  169.3 0.0 copy-done.8
  169.3 0.0 copy-start.6
  169.3 0.7 copy-done.6
  170.0 26.8 %gather.1 = f32[8,240,128]{2,1,0:T(8,128)} custom-call(bf16[1920,1024]{1,0:T(8,128)(2,1)} %copy-done.2, f32[64,1920]{1,0:T(8,128)S(1)} %reshape.22.exp_ref, bf16[64,1920]{1,0:T(8,128)(2,1)} %collective-permute-done.rest_0_, bf16[64,1920]{1,0:T(8,128)(2,1)} %collective-permute-done.1.rest_1_, bf16[64,1920]{1,0:T(8,128)(2,1)} %collective-permute-done.2.rest_2_, ...), custom_call_target="tpu_custom_call" | custom-call | tf_op jit(solution)/shard_map/gather/pallas_call | solution.py:230
  (4 shorter events, 0.0 us)
Async XLA Ops:
  6.5 24.5 %copy-start.10 = (s32[128]{0:T(128)S(1)}, s32[128]{0:T(128)}, u32[]{:S(2)}) copy-start(s32[128]{0:T(128)} %param.21) | copy-start | bytes 1540
  6.5 24.5 %copy-start.13 = (f32[64,64]{1,0:T(8,128)S(1)}, f32[64,64]{1,0:T(8,128)}, u32[]{:S(2)}) copy-start(f32[64,64]{1,0:T(8,128)} %param.20) | copy-start | bytes 49156
  6.5 24.6 %copy-start.14 = (f32[2,240]{1,0:T(2,128)S(1)}, f32[2,240]{1,0:T(2,128)}, u32[]{:S(2)}) copy-start(f32[2,240]{1,0:T(2,128)} %param.15) | copy-start | bytes 5764
  6.5 87.9 %all-reduce.3.cloned.1.call-start = ((), (), s32[]{:S(2)}) async-start(), calls=%async_computation | async-start | bytes 245760
  7.4 1.2 copy-start
  8.6 1.2 copy-start.3
  9.8 0.7 copy-start.7
  10.5 0.7 copy-start.9
  11.2 19.1 %copy-start.12 = (bf16[2,240,240]{2,1,0:T(8,128)(2,1)S(1)}, bf16[2,240,240]{2,1,0:T(8,128)(2,1)}, u32[]{:S(2)}) copy-start(bf16[2,240,240]{2,1,0:T(8,128)(2,1)} %param.19) | copy-start | bytes 691204
  11.2 20.1 %copy-start.11 = (bf16[3,2,240,240]{3,2,1,0:T(8,128)(2,1)S(1)}, bf16[3,2,240,240]{3,2,1,0:T(8,128)(2,1)}, u32[]{:S(2)}) copy-start(bf16[3,2,240,240]{3,2,1,0:T(8,128)(2,1)} %param.17) | copy-start | bytes 2073604
  15.8 1.9 copy-start.2
  17.7 23.4 %collective-permute-start = (bf16[64,1920]{1,0:T(8,128)(2,1)S(1)}, bf16[64,1920]{1,0:T(8,128)(2,1)}, u32[]{:S(2)}, u32[]{:S(2)}) collective-permute-start(bf16[64,1920]{1,0:T(8,128)(2,1)S(1)} %get-tuple-element.15), channel_id=1, source_target_pairs={{0,1},{1,2},{2,3},{3,4},{4,5},{5,6},{6,7},{7,0},{8,9},{9,10},{10,1... | collective-permute-start | bytes 737288 | tf_op jit(solution)/shard_map/ppermute | solution.py:17
  20.7 148.5 %collective-permute-start.1 = (bf16[64,1920]{1,0:T(8,128)(2,1)}, bf16[64,1920]{1,0:T(8,128)(2,1)}, u32[]{:S(2)}, u32[]{:S(2)}) collective-permute-start(bf16[64,1920]{1,0:T(8,128)(2,1)} %get-tuple-element.16), channel_id=1, source_target_pairs={{0,7},{1,0},{2,1},{3,2},{4,3},{5,4},{6,5},{7,6},{8,15},{9,8},{10,9... | collective-permute-start | bytes 737288 | tf_op jit(solution)/shard_map/ppermute | solution.py:17
  23.8 145.4 %collective-permute-start.2 = (bf16[64,1920]{1,0:T(8,128)(2,1)}, bf16[64,1920]{1,0:T(8,128)(2,1)}, u32[]{:S(2)}, u32[]{:S(2)}) collective-permute-start(bf16[64,1920]{1,0:T(8,128)(2,1)} %get-tuple-element.17), channel_id=1, source_target_pairs={{0,2},{1,3},{2,4},{3,5},{4,6},{5,7},{6,0},{7,1},{8,10},{9,11},{10,... | collective-permute-start | bytes 737288 | tf_op jit(solution)/shard_map/ppermute | solution.py:17
  23.8 145.5 %collective-permute-start.3 = (bf16[64,1920]{1,0:T(8,128)(2,1)}, bf16[64,1920]{1,0:T(8,128)(2,1)}, u32[]{:S(2)}, u32[]{:S(2)}) collective-permute-start(bf16[64,1920]{1,0:T(8,128)(2,1)} %get-tuple-element.18), channel_id=1, source_target_pairs={{0,6},{1,7},{2,0},{3,1},{4,2},{5,3},{6,4},{7,5},{8,14},{9,15},{10,... | collective-permute-start | bytes 737288 | tf_op jit(solution)/shard_map/ppermute | solution.py:17
  27.6 141.6 %collective-permute-start.4 = (bf16[64,1920]{1,0:T(8,128)(2,1)}, bf16[64,1920]{1,0:T(8,128)(2,1)}, u32[]{:S(2)}, u32[]{:S(2)}) collective-permute-start(bf16[64,1920]{1,0:T(8,128)(2,1)} %get-tuple-element.19), channel_id=1, source_target_pairs={{0,8},{8,16},{16,24},{24,0},{1,9},{9,17},{17,25},{25,1},{2,10},{10... | collective-permute-start | bytes 737288 | tf_op jit(solution)/shard_map/ppermute | solution.py:17
  33.1 3.6 %copy-start.1 = (bf16[8,240,240]{2,1,0:T(8,128)(2,1)S(1)}, bf16[8,240,240]{2,1,0:T(8,128)(2,1)}, u32[]{:S(2)}) copy-start(bf16[8,240,240]{2,1,0:T(8,128)(2,1)} %rot_ref.1) | copy-start | bytes 2764804
  36.8 132.5 %copy-start.4 = (f32[8,240,128]{2,1,0:T(8,128)S(1)}, f32[8,240,128]{2,1,0:T(8,128)}, u32[]{:S(2)}) copy-start(f32[8,240,128]{2,1,0:T(8,128)} %rest_12_.1) | copy-start | bytes 2949124
  36.8 132.5 %copy-start.5 = (s32[24,128]{1,0:T(8,128)S(1)}, s32[24,128]{1,0:T(8,128)}, u32[]{:S(2)}) copy-start(s32[24,128]{1,0:T(8,128)} %rest_15_.1) | copy-start | bytes 36868
  36.8 132.5 %copy-start.8 = (s32[128]{0:T(128)S(1)}, s32[128]{0:T(128)}, u32[]{:S(2)}) copy-start(s32[128]{0:T(128)} %param.22) | copy-start | bytes 1540
  41.1 128.1 %collective-permute-start.5 = (bf16[64,1920]{1,0:T(8,128)(2,1)}, bf16[64,1920]{1,0:T(8,128)(2,1)}, u32[]{:S(2)}, u32[]{:S(2)}) collective-permute-start(bf16[64,1920]{1,0:T(8,128)(2,1)} %get-tuple-element.20), channel_id=1, source_target_pairs={{0,24},{8,0},{16,8},{24,16},{1,25},{9,1},{17,9},{25,17},{2,26},{10... | collective-permute-start | bytes 737288 | tf_op jit(solution)/shard_map/ppermute | solution.py:17
  169.3 0.7 copy-start.6
Sparse Core Ops, SparseCore 0:
  17.8 76.6 all-reduce.2

commit v2 on v1

--- a/solution.py
+++ b/solution.py
@@ -12,9 +12,88 @@
 MIB = 1 << 20
 
 
-def shifted(value, axis, by):
-    length = lax.axis_size(axis)
-    return lax.ppermute(value, axis, [(i, (i + by) % length) for i in range(length)])
+MESH = pl.DeviceIdType.MESH
+MEM_MOVES = (1, -1, 2, -2)
+GRP_MOVES = (1, -1)
+
+
+def exchange_kernel(peers, n_grp, n_mem, *refs):
+    out_refs = refs[:peers]
+    sums_ref = refs[peers]
+    recv_refs = refs[peers + 1 : 2 * peers + 1]
+    exp_ref = refs[2 * peers + 1]
+    parts, near_s, near_r, red_s, red_r, grp_s, grp_r, mem_s, mem_r = refs[2 * peers + 2 :]
+    g = lax.axis_index("grp")
+    m = lax.axis_index("mem")
+
+    def mem_peer(by):
+        return (g, lax.rem(m + by + n_mem, n_mem))
+
+    def grp_peer(by):
+        return (lax.rem(g + by + n_grp, n_grp), m)
+
+    def copy(src, dst, send, recv, device):
+        return pltpu.make_async_remote_copy(
+            src_ref=src, dst_ref=dst, send_sem=send, recv_sem=recv,
+            device_id=device, device_id_type=MESH,
+        )
+
+    everyone = [mem_peer(k) for k in range(1, n_mem)] + [grp_peer(k) for k in range(1, n_grp)]
+    barrier = pltpu.get_barrier_semaphore()
+    for device in everyone:
+        pl.semaphore_signal(barrier, inc=1, device_id=device, device_id_type=MESH)
+    pl.semaphore_wait(barrier, len(everyone))
+
+    reduce_copies = []
+    for k in range(1, n_mem):
+        device = mem_peer(k)
+        reduce_copies.append(
+            copy(sums_ref.at[device[1]], parts.at[k - 1], red_s.at[k - 1], red_r.at[k - 1], device)
+        )
+    near_peers = [mem_peer(by) for by in MEM_MOVES] + [grp_peer(by) for by in GRP_MOVES]
+    near_copies = [
+        copy(out_refs[p], recv_refs[p], near_s.at[p], near_r.at[p], near_peers[p])
+        for p in range(peers)
+    ]
+    for c in reduce_copies + near_copies:
+        c.start()
+    for c in reduce_copies:
+        c.wait_recv()
+    share = sums_ref[m]
+    for k in range(1, n_mem):
+        share = share + parts[k - 1]
+    exp_ref[m, g] = share
+    grp_copies = [
+        copy(exp_ref.at[m, g], exp_ref.at[m, g], grp_s.at[k - 1], grp_r.at[k - 1], grp_peer(k))
+        for k in range(1, n_grp)
+    ]
+    for c in grp_copies:
+        c.start()
+    for c in grp_copies:
+        c.wait_recv()
+    mem_copies = [
+        copy(exp_ref.at[m], exp_ref.at[m], mem_s.at[k - 1], mem_r.at[k - 1], mem_peer(k))
+        for k in range(1, n_mem)
+    ]
+    for c in mem_copies:
+        c.start()
+    for c in near_copies + mem_copies:
+        c.wait_recv()
+    for c in reduce_copies + near_copies + grp_copies + mem_copies:
+        c.wait_send()
+
+
+def pair_apply(pair, wide):
+    n_coef = pair.shape[1]
+    half = wide.shape[1] // 2
+    return pair_combine(dot_nn(pair.reshape(2 * n_coef, n_coef), wide), n_coef, half)
+
+
+def pair_combine(acc, n_coef, half):
+    return (
+        acc[:n_coef, :half] - acc[n_coef:, half:],
+        acc[:n_coef, half:] + acc[n_coef:, :half],
+    )
 
 
 def dot_nn(a, b):
@@ -32,7 +111,8 @@
     comps, n_coef, sph = coef_ref.shape
     rots = rot_ref.shape[0]
     pool = rots * sph
-    group = sums_ref.shape[0]
+    members, each = sums_ref.shape[0], sums_ref.shape[1]
+    group = members * each
     x_all = jnp.concatenate([coef_ref[x].astype(BF16) for x in range(comps)], axis=1)
     for r in range(rots):
         turned = dot_nn(rot_ref[r], x_all).astype(BF16)
@@ -54,7 +134,9 @@
         picked = dot_nt(sel[...], pool_ref[at : at + step, :])
         for p in range(peers):
             out_refs[p][:, at : at + step] = picked[p * width : (p + 1) * width].astype(BF16)
-        sums_ref[:, at : at + step] = picked[total:]
+        for q in range(members):
+            row = total + q * each
+            sums_ref[q, :, at : at + step] = picked[row : row + each]
 
 
 def gather_kernel(
@@ -102,19 +184,16 @@
         exp_ref[...].T, weights, precision=lax.Precision.HIGHEST, preferred_element_type=F32
     )
     folded = jnp.concatenate(
-        [
-            jnp.concatenate(
-                [near_sum[(c * dirs + d) * n_coef : (c * dirs + d + 1) * n_coef] for d in range(dirs)],
-                axis=1,
-            )
-            for c in range(2)
-        ],
-        axis=0,
+        [near_sum[x * n_coef : (x + 1) * n_coef] for x in range(comps)], axis=1
     )
     high = folded.astype(BF16)
     low = (folded - high.astype(F32)).astype(BF16)
-    reached = dot_nn(up_ref[...], high) + dot_nn(up_ref[...], low)
-    far_s[...] = dot_nn(far_ref[...], reached.astype(BF16))
+    high_re, high_im = pair_apply(up_ref[...], high)
+    low_re, low_im = pair_apply(up_ref[...], low)
+    reached = jnp.concatenate([high_re + low_re, high_im + low_im], axis=1).astype(BF16)
+    far_re, far_im = pair_apply(far_ref[...], reached)
+    far_s[:, :half] = far_re
+    far_s[:, half:] = far_im
 
     j_iota = lax.broadcasted_iota(jnp.int32, (sph, sph), 0)
 
@@ -131,18 +210,18 @@
         sel_s[sph:, :] = jnp.where(mine, count_s[...].astype(F32), 0.0).astype(BF16)
         sel = sel_s[...]
         for x in range(comps):
-            c, d = x // dirs, x % dirs
             rows = slice(x * n_coef, (x + 1) * n_coef)
             lhs = jnp.concatenate([pool_ref[rows, pl.ds(first, sph)], recv_s[rows, :]], axis=1)
             taken = dot_nn(lhs, sel).astype(BF16)
             for h in range(shells):
-                at = (h * 2 + c) * n_coef
-                taken_s[at : at + n_coef, d * sph : (d + 1) * sph] = taken[:, h * sph : (h + 1) * sph]
-        moved = dot_nn(axial_ref[...], taken_s[...])
+                taken_s[h, :, x * sph : (x + 1) * sph] = taken[:, h * sph : (h + 1) * sph]
+        acc = dot_nn(axial_ref[0].reshape(2 * n_coef, n_coef), taken_s[0])
+        for h in range(1, shells):
+            acc = acc + dot_nn(axial_ref[h].reshape(2 * n_coef, n_coef), taken_s[h])
+        moved_re, moved_im = pair_combine(acc, n_coef, half)
         here = jnp.concatenate([crot_ref[...]] * dirs, axis=1) == r
-        summed = (moved + jnp.where(here, far_s[...], 0.0)).astype(BF16)
-        gath_s[r, :, :half] = summed[:n_coef]
-        gath_s[r, :, half:] = summed[n_coef:]
+        gath_s[r, :, :half] = (moved_re + jnp.where(here, far_s[:, :half], 0.0)).astype(BF16)
+        gath_s[r, :, half:] = (moved_im + jnp.where(here, far_s[:, half:], 0.0)).astype(BF16)
 
     field = dot_nn(rott_ref[...], gath_s[...].reshape(rots * n_coef, comps * sph))
     mie_r = mie_ref[:, 0:1]
@@ -152,16 +231,6 @@
         im = inc_ref[dirs + d] + field[:, half + d * sph : half + (d + 1) * sph]
         out_ref[d] = mie_r * re - mie_i * im
         out_ref[dirs + d] = mie_r * im + mie_i * re
-
-
-def complex_block(pair):
-    return jnp.concatenate(
-        [
-            jnp.concatenate([pair[..., 0, :, :], -pair[..., 1, :, :]], axis=-1),
-            jnp.concatenate([pair[..., 1, :, :], pair[..., 0, :, :]], axis=-1),
-        ],
-        axis=-2,
-    )
 
 
 def on_device(
@@ -184,12 +253,13 @@
     pool = rots * sph
     rows = comps * n_coef
     clus = coupling.shape[0]
-    group = clus // lax.axis_size("grp")
+    n_grp, n_mem = lax.axis_size("grp"), lax.axis_size("mem")
+    group = clus // n_grp
+    each = group // n_mem
     peers, width = send_col.shape
     total = peers * width
     shells = axial_shells.shape[0]
     per_shell = pair_col.shape[0] // shells
-    dirs = comps // 2
     vmem = pl.BlockSpec(memory_space=pltpu.VMEM)
     clus_row = cluster_ids.reshape(1, sph)
     crot_row = center_rot.reshape(1, sph)
@@ -198,7 +268,7 @@
         functools.partial(rotate_kernel, peers, width),
         out_shape=[
             jax.ShapeDtypeStruct((rows, pool), BF16),
-            jax.ShapeDtypeStruct((group, rows), F32),
+            jax.ShapeDtypeStruct((n_mem, each, rows), F32),
         ]
         + [jax.ShapeDtypeStruct((width, rows), BF16)] * peers,
         in_specs=[vmem] * 5,
@@ -209,24 +279,31 @@
     )(coefficients, rot_table, send_col.reshape(total, 1), clus_row, crot_row)
     rotated, sums = first[0], first[1]
     outgoing = first[2:]
-    shares = lax.psum_scatter(sums, "mem", scatter_dimension=0, tiled=True)
-    expansions = lax.all_gather(shares, ("grp", "mem"), axis=0, tiled=True)
-    mem_moves = [1, -1, 2, -2]
-    grp_moves = [1, -1]
-    received = [shifted(outgoing[i], "mem", by) for i, by in enumerate(mem_moves)]
-    received += [
-        shifted(outgoing[len(mem_moves) + i], "grp", by) for i, by in enumerate(grp_moves)
-    ]
-
-    axial = complex_block(axial_shells)
-    axial = jnp.transpose(axial, (1, 0, 2)).reshape(2 * n_coef, shells * 2 * n_coef)
-    up = complex_block(up_axial)
-    far = complex_block(far_axial)
+    dma = pltpu.SemaphoreType.DMA
+    exchanged = pl.pallas_call(
+        functools.partial(exchange_kernel, peers, n_grp, n_mem),
+        out_shape=[jax.ShapeDtypeStruct((width, rows), BF16)] * peers
+        + [jax.ShapeDtypeStruct((n_mem, n_grp, each, rows), F32)],
+        in_specs=[vmem] * (peers + 1),
+        out_specs=[vmem] * (peers + 1),
+        scratch_shapes=[pltpu.VMEM((n_mem - 1, each, rows), F32)]
+        + [dma((peers,))] * 2
+        + [dma((n_mem - 1,))] * 2
+        + [dma((n_grp - 1,))] * 2
+        + [dma((n_mem - 1,))] * 2,
+        compiler_params=pltpu.CompilerParams(
+            collective_id=0, has_side_effects=True, vmem_limit_bytes=32 * MIB
+        ),
+        name="exchange",
+    )(*outgoing, sums)
+    received = exchanged[:peers]
+    expansions = exchanged[peers].reshape(clus, rows)
+
     rott = jnp.transpose(rot_table, (2, 0, 1)).reshape(n_coef, rots * n_coef)
     eye = jnp.arange(clus)[:, None] == jnp.arange(clus)[None, :]
     coup_t = jnp.where(eye, F32(0.0), coupling).T
+    coup_t = coup_t.reshape(n_grp, n_mem, each, clus).transpose(1, 0, 2, 3).reshape(clus, clus)
     gid = clus_row + lax.axis_index("grp") * group
-    half = dirs * sph
     return pl.pallas_call(
         functools.partial(gather_kernel, peers, per_shell),
         out_shape=jax.ShapeDtypeStruct((comps, n_coef, sph), F32),
@@ -236,14 +313,14 @@
             pltpu.VMEM((rows, total), BF16),
             pltpu.VMEM((total, shells * sph), BF16),
             pltpu.VMEM((sph + total, shells * sph), BF16),
-            pltpu.VMEM((shells * 2 * n_coef, half), BF16),
-            pltpu.VMEM((2 * n_coef, half), F32),
+            pltpu.VMEM((shells, n_coef, comps * sph), BF16),
+            pltpu.VMEM((n_coef, comps * sph), F32),
             pltpu.VMEM((rots, n_coef, comps * sph), BF16),
         ],
         compiler_params=pltpu.CompilerParams(vmem_limit_bytes=48 * MIB),
         name="gather",
     )(
-        rotated, expansions, *received, coup_t, axial, up, far, rott, mie_coeffs.T, incident,
+        rotated, expansions, *received, coup_t, axial_shells, up_axial, far_axial, rott, mie_coeffs.T, incident,
         gid, crot_row, pair_col, pair_rot,
     )
 

time: 204 us -> 85.2 us (0.42)
  blocking collectives: 72.5 us -> 0 us
  waiting for transfers between devices: 51.6 us -> 0 us
  Pallas kernels: 31.4 us -> 62.8 us
  between operations: 14.2 us -> 0.2 us
  starting transfers between devices: 11.7 us -> 0 us
  other arithmetic: 5.15 us -> 0.01 us
  local copies, waits for them, and re-layouts: 17 us -> 20.7 us
    all_gather x1 -> x0, blocking collectives: 72.5 us -> none  [on_device(): expansions = lax.all_gather(shares, ('grp', 'mem'), axis=0, tiled=True)]
    unnamed x2 -> x0, waiting for transfers between devices: 51.5 us -> none
    pallas_call x0 -> x1, Pallas kernels: none -> 33.5 us  [on_device(): pl.pallas_call(functools.partial(exchange_kernel, peers, n_grp, n_mem), o...]
    ppermute x6 -> x0, starting transfers between devices: 11.7 us -> none  [shifted(): lax.ppermute(value, axis, [(i, (i + by) % length) for i in range(length)])]
    unnamed x37 -> x58, local copies, waits for them, and re-layouts: 11 us -> 18.7 us
    concatenate x2 -> x0, other arithmetic: 3.45 us -> none  [complex_block(): jnp.concatenate([jnp.concatenate([pair[..., 0, :, :], -pair[..., 1, :, :]...]
    squeeze x2 -> x0, local copies, waits for them, and re-layouts: 2.45 us -> none  [complex_block(): pair[..., 1, :, :]]
  transfers between devices with their start and end apart: 7 -> 0, of which waited for: 1 -> 0; matrix products, arithmetic and copies ran while one was open for 7% -> 0% of each run, Pallas kernels for 0% -> 0%
where the time goes in v2:
time: 85.2 us; the launch traced here: 83.7 us
  Pallas kernels  62.8 us (74%)
  local copies, waits for them, and re-layouts  20.7 us (24%)
    pallas_call x1, Pallas kernels, on_device(): pl.pallas_call(functools.partial(exchange_kernel, peers, n_grp, n_mem), o...  33.5 us
    pallas_call x1, Pallas kernels, on_device(): pl.pallas_call(functools.partial(gather_kernel, peers, per_shell), out_sh...  25.7 us
    unnamed x58, local copies, waits for them, and re-layouts  18.7 us
    pallas_call x1, Pallas kernels, on_device(): pl.pallas_call(functools.partial(rotate_kernel, peers, width), out_shape=...  3.57 us

profile of v2, /device:TPU:0, one launch (start us, length us, event | category | flops | bytes accessed | tf_op | source)
XLA Modules:
  0.0 83.7 jit_solution(6442550847574169415)
XLA Ops:
  0.0 0.0 copy-start.23
  0.0 0.0 copy-start.25
  0.0 0.0 copy-start.27
  0.0 0.0 copy-start.26
  0.0 0.0 copy-start.20
  0.0 0.0 copy-start.21
  0.0 0.9 %reshape.29.send_ref = s32[384,1]{1,0:T(8,128)S(1)} reshape(s32[6,64]{1,0:T(8,128)} %param.25) | data formatting | bytes 3072 | tf_op jit(solution)/shard_map/reshape | solution.py:279
  0.9 0.0 copy-start.1
  0.9 1.2 %copy-done.1 = bf16[8,240,240]{2,1,0:T(8,128)(2,1)S(1)} copy-done((bf16[8,240,240]{2,1,0:T(8,128)(2,1)S(1)}, bf16[8,240,240]{2,1,0:T(8,128)(2,1)}, u32[]{:S(2)}) %copy-start.1) | copy-done | bytes 921624
  2.1 0.0 copy-start.3
  2.1 1.2 %copy-done.3 = f32[8,240,128]{2,1,0:T(8,128)S(1)} copy-done((f32[8,240,128]{2,1,0:T(8,128)S(1)}, f32[8,240,128]{2,1,0:T(8,128)}, u32[]{:S(2)}) %copy-start.3) | copy-done | bytes 983064
  3.3 0.0 copy-start.22
  3.3 0.7 copy-done.22
  4.0 0.0 copy-start.24
  4.0 0.7 copy-done.24
  4.6 0.0 copy-start.2
  4.6 0.0 copy-start.4
  4.6 3.6 %rotate.1 = (bf16[1920,1024]{1,0:T(8,128)(2,1)S(1)}, f32[8,2,1920]{2,1,0:T(2,128)S(1)}, bf16[64,1920]{1,0:T(8,128)(2,1)S(1)}, bf16[64,1920]{1,0:T(8,128)(2,1)S(1...) custom-call(f32[8,240,128]{2,1,0:T(8,128)S(1)} %copy-done.3, ...), custom_call_target="tpu_custom_call" | custom-call | tf_op jit(solution)/shard_map/rotate/pallas_call | solution.py:267
  8.2 0.0 copy-start
  8.2 1.9 %copy-done = bf16[1920,1024]{1,0:T(8,128)(2,1)} copy-done((bf16[1920,1024]{1,0:T(8,128)(2,1)}, bf16[1920,1024]{1,0:T(8,128)(2,1)S(1)}, u32[]{:S(2)}) %copy-start) | copy-done | bytes 3932184
  10.1 33.5 %exchange.1 = (bf16[64,1920]{1,0:T(8,128)(2,1)S(1)}, bf16[64,1920]{1,0:T(8,128)(2,1)S(1)}, bf16[64,1920]{1,0:T(8,128)(2,1)S(1)}, bf16[64,1920]{1,0:T(8,128)(2,1)...) custom-call(bf16[64,1920]{1,0:T(8,128)(2,1)S(1)} %get-tuple-element.21.refs_0_, ...), custom_call_target="tpu_custom_call" | custom-call | tf_op jit(solution)/shard_map/exchange/pallas_call | solution.py:283
  43.6 0.0 copy-start.8
  43.6 0.7 copy-done.8
  44.3 0.0 copy-start.10
  44.3 0.7 copy-done.10
  45.0 0.0 copy-start.12
  45.0 0.7 copy-done.12
  45.7 0.0 copy-start.14
  45.7 0.7 copy-done.14
  46.4 0.0 copy-start.16
  46.4 0.7 copy-done.16
  47.1 0.0 copy-start.18
  47.1 0.7 copy-done.18
  47.8 0.3 reshape.25.exp_ref
  48.1 0.0 copy-done.2
  48.2 0.8 %copy.22.rest_10_ = bf16[240,1920]{1,0:T(8,128)(2,1)S(1)} copy(bf16[240,1920]{0,1:T(8,128)(2,1)S(1)} %bitcast.14) | data formatting | bytes 1843200 | tf_op jit(solution)/shard_map/reshape | solution.py:302
  49.0 0.0 copy-done.27
  49.0 0.1 copy.21
  49.2 0.0 copy-done.26
  49.2 0.1 copy.18
  49.3 0.0 copy-done.25
  49.3 0.0 copy-done.23
  49.3 0.0 copy-done.20
  49.3 0.0 copy-done.21
  49.3 0.0 copy-done.4
  49.4 0.0 copy-start.5
  49.4 1.1 %copy-done.5 = bf16[3,2,240,240]{3,2,1,0:T(8,128)(2,1)S(1)} copy-done((bf16[3,2,240,240]{3,2,1,0:T(8,128)(2,1)S(1)}, bf16[3,2,240,240]{3,2,1,0:T(8,128)(2,1)}, u32[]{:S(2)}) %copy-start.5) | copy-done | bytes 691224
  50.5 0.0 copy-start.6
  50.5 0.9 %copy-done.6 = bf16[2,240,240]{2,1,0:T(8,128)(2,1)S(1)} copy-done((bf16[2,240,240]{2,1,0:T(8,128)(2,1)S(1)}, bf16[2,240,240]{2,1,0:T(8,128)(2,1)}, u32[]{:S(2)}) %copy-start.6) | copy-done | bytes 230424
  51.4 0.0 copy-start.7
  51.4 0.9 %copy-done.7 = bf16[2,240,240]{2,1,0:T(8,128)(2,1)S(1)} copy-done((bf16[2,240,240]{2,1,0:T(8,128)(2,1)S(1)}, bf16[2,240,240]{2,1,0:T(8,128)(2,1)}, u32[]{:S(2)}) %copy-start.7) | copy-done | bytes 230424
  52.4 0.0 copy-start.9
  52.4 0.9 %copy-done.9 = bf16[64,1920]{1,0:T(8,128)(2,1)S(1)} copy-done((bf16[64,1920]{1,0:T(8,128)(2,1)S(1)}, bf16[64,1920]{1,0:T(8,128)(2,1)}, u32[]{:S(2)}) %copy-start.9) | copy-done | bytes 245784
  53.3 0.0 copy-start.11
  53.3 0.9 %copy-done.11 = bf16[64,1920]{1,0:T(8,128)(2,1)S(1)} copy-done((bf16[64,1920]{1,0:T(8,128)(2,1)S(1)}, bf16[64,1920]{1,0:T(8,128)(2,1)}, u32[]{:S(2)}) %copy-start.11) | copy-done | bytes 245784
  54.2 0.0 copy-start.13
  54.3 0.9 %copy-done.13 = bf16[64,1920]{1,0:T(8,128)(2,1)S(1)} copy-done((bf16[64,1920]{1,0:T(8,128)(2,1)S(1)}, bf16[64,1920]{1,0:T(8,128)(2,1)}, u32[]{:S(2)}) %copy-start.13) | copy-done | bytes 245784
  55.2 0.0 copy-start.15
  55.2 0.9 %copy-done.15 = bf16[64,1920]{1,0:T(8,128)(2,1)S(1)} copy-done((bf16[64,1920]{1,0:T(8,128)(2,1)S(1)}, bf16[64,1920]{1,0:T(8,128)(2,1)}, u32[]{:S(2)}) %copy-start.15) | copy-done | bytes 245784
  56.1 0.0 copy-start.17
  56.1 0.9 %copy-done.17 = bf16[64,1920]{1,0:T(8,128)(2,1)S(1)} copy-done((bf16[64,1920]{1,0:T(8,128)(2,1)S(1)}, bf16[64,1920]{1,0:T(8,128)(2,1)}, u32[]{:S(2)}) %copy-start.17) | copy-done | bytes 245784
  57.1 0.0 copy-start.19
  57.1 0.9 %copy-done.19 = bf16[64,1920]{1,0:T(8,128)(2,1)S(1)} copy-done((bf16[64,1920]{1,0:T(8,128)(2,1)S(1)}, bf16[64,1920]{1,0:T(8,128)(2,1)}, u32[]{:S(2)}) %copy-start.19) | copy-done | bytes 245784
  58.0 25.7 %gather.1 = f32[8,240,128]{2,1,0:T(8,128)} custom-call(bf16[1920,1024]{1,0:T(8,128)(2,1)} %copy-done, f32[64,1920]{1,0:T(8,128)S(1)} %reshape.25.exp_ref, bf16[64,1920]{1,0:T(8,128)(2,1)S(1)} %copy-done.9, bf16[64,1920]{1,0:T(8,128)(2,1)S(1)} %copy-done.11, bf16[64,1920]{1,0:T(8,128)(2,1)S(1)} %copy-done.13, bf16[64,1920]{1,0:T(8,128)(2,1)S(1)} %copy-done.15, ...), custom_call_target="tpu_custom_call" | custom-call | tf_op jit(solution)/shard_map/gather/pallas_call | solution.py:307
  (3 shorter events, 0.0 us)
Async XLA Ops:
  0.0 49.3 %copy-start.23 = (s32[128]{0:T(128)S(1)}, s32[128]{0:T(128)}, u32[]{:S(2)}) copy-start(s32[128]{0:T(128)} %param.22) | copy-start | bytes 1540
  0.0 49.3 %copy-start.25 = (s32[128]{0:T(128)S(1)}, s32[128]{0:T(128)}, u32[]{:S(2)}) copy-start(s32[128]{0:T(128)} %param.21) | copy-start | bytes 1540
  0.0 49.0 %copy-start.27 = (f32[2,240]{1,0:T(2,128)S(1)}, f32[2,240]{1,0:T(2,128)}, u32[]{:S(2)}) copy-start(f32[2,240]{1,0:T(2,128)} %param.15) | copy-start | bytes 5764
  0.0 49.2 %copy-start.26 = (f32[64,64]{1,0:T(8,128)S(1)}, f32[64,64]{1,0:T(8,128)}, u32[]{:S(2)}) copy-start(f32[64,64]{1,0:T(8,128)} %param.20) | copy-start | bytes 49156
  0.0 49.3 %copy-start.20 = (s32[24,128]{1,0:T(8,128)S(1)}, s32[24,128]{1,0:T(8,128)}, u32[]{:S(2)}) copy-start(s32[24,128]{1,0:T(8,128)} %rest_15_.1) | copy-start | bytes 36868
  0.0 49.3 %copy-start.21 = (s32[24,128]{1,0:T(8,128)S(1)}, s32[24,128]{1,0:T(8,128)}, u32[]{:S(2)}) copy-start(s32[24,128]{1,0:T(8,128)} %rest_16_.1) | copy-start | bytes 36868
  0.9 1.2 %copy-start.1 = (bf16[8,240,240]{2,1,0:T(8,128)(2,1)S(1)}, bf16[8,240,240]{2,1,0:T(8,128)(2,1)}, u32[]{:S(2)}) copy-start(bf16[8,240,240]{2,1,0:T(8,128)(2,1)} %rot_ref.1) | copy-start | bytes 2764804
  2.1 1.2 %copy-start.3 = (f32[8,240,128]{2,1,0:T(8,128)S(1)}, f32[8,240,128]{2,1,0:T(8,128)}, u32[]{:S(2)}) copy-start(f32[8,240,128]{2,1,0:T(8,128)} %coef_ref.1) | copy-start | bytes 2949124
  3.3 0.7 copy-start.22
  4.0 0.7 copy-start.24
  4.6 43.5 %copy-start.2 = (bf16[8,240,240]{2,1,0:T(8,128)(2,1)S(1)}, bf16[8,240,240]{2,1,0:T(8,128)(2,1)}, u32[]{:S(2)}) copy-start(bf16[8,240,240]{2,1,0:T(8,128)(2,1)} %rot_ref.1) | copy-start | bytes 2764804
  4.6 44.7 %copy-start.4 = (f32[8,240,128]{2,1,0:T(8,128)S(1)}, f32[8,240,128]{2,1,0:T(8,128)}, u32[]{:S(2)}) copy-start(f32[8,240,128]{2,1,0:T(8,128)} %rest_12_.1) | copy-start | bytes 2949124
  8.2 1.9 %copy-start = (bf16[1920,1024]{1,0:T(8,128)(2,1)}, bf16[1920,1024]{1,0:T(8,128)(2,1)S(1)}, u32[]{:S(2)}) copy-start(bf16[1920,1024]{1,0:T(8,128)(2,1)S(1)} %get-tuple-element.20.pool_ref) | copy-start | bytes 11796484
  43.6 0.7 copy-start.8
  44.3 0.7 copy-start.10
  45.0 0.7 copy-start.12
  45.7 0.7 copy-start.14
  46.4 0.7 copy-start.16
  47.1 0.7 copy-start.18
  49.4 1.1 %copy-start.5 = (bf16[3,2,240,240]{3,2,1,0:T(8,128)(2,1)S(1)}, bf16[3,2,240,240]{3,2,1,0:T(8,128)(2,1)}, u32[]{:S(2)}) copy-start(bf16[3,2,240,240]{3,2,1,0:T(8,128)(2,1)} %rest_7_.1) | copy-start | bytes 2073604
  50.5 0.9 %copy-start.6 = (bf16[2,240,240]{2,1,0:T(8,128)(2,1)S(1)}, bf16[2,240,240]{2,1,0:T(8,128)(2,1)}, u32[]{:S(2)}) copy-start(bf16[2,240,240]{2,1,0:T(8,128)(2,1)} %rest_8_.1) | copy-start | bytes 691204
  51.4 0.9 %copy-start.7 = (bf16[2,240,240]{2,1,0:T(8,128)(2,1)S(1)}, bf16[2,240,240]{2,1,0:T(8,128)(2,1)}, u32[]{:S(2)}) copy-start(bf16[2,240,240]{2,1,0:T(8,128)(2,1)} %rest_9_.1) | copy-start | bytes 691204
  52.4 0.9 %copy-start.9 = (bf16[64,1920]{1,0:T(8,128)(2,1)S(1)}, bf16[64,1920]{1,0:T(8,128)(2,1)}, u32[]{:S(2)}) copy-start(bf16[64,1920]{1,0:T(8,128)(2,1)} %copy-done.8) | copy-start | bytes 737284
  53.3 0.9 %copy-start.11 = (bf16[64,1920]{1,0:T(8,128)(2,1)S(1)}, bf16[64,1920]{1,0:T(8,128)(2,1)}, u32[]{:S(2)}) copy-start(bf16[64,1920]{1,0:T(8,128)(2,1)} %copy-done.10) | copy-start | bytes 737284
  54.2 0.9 %copy-start.13 = (bf16[64,1920]{1,0:T(8,128)(2,1)S(1)}, bf16[64,1920]{1,0:T(8,128)(2,1)}, u32[]{:S(2)}) copy-start(bf16[64,1920]{1,0:T(8,128)(2,1)} %copy-done.12) | copy-start | bytes 737284
  55.2 0.9 %copy-start.15 = (bf16[64,1920]{1,0:T(8,128)(2,1)S(1)}, bf16[64,1920]{1,0:T(8,128)(2,1)}, u32[]{:S(2)}) copy-start(bf16[64,1920]{1,0:T(8,128)(2,1)} %copy-done.14) | copy-start | bytes 737284
  56.1 0.9 %copy-start.17 = (bf16[64,1920]{1,0:T(8,128)(2,1)S(1)}, bf16[64,1920]{1,0:T(8,128)(2,1)}, u32[]{:S(2)}) copy-start(bf16[64,1920]{1,0:T(8,128)(2,1)} %copy-done.16) | copy-start | bytes 737284
  57.1 0.9 %copy-start.19 = (bf16[64,1920]{1,0:T(8,128)(2,1)S(1)}, bf16[64,1920]{1,0:T(8,128)(2,1)}, u32[]{:S(2)}) copy-start(bf16[64,1920]{1,0:T(8,128)(2,1)} %copy-done.18) | copy-start | bytes 737284

commit v3 on v2

--- a/solution.py
+++ b/solution.py
@@ -17,12 +17,16 @@
 GRP_MOVES = (1, -1)
 
 
-def exchange_kernel(peers, n_grp, n_mem, *refs):
-    out_refs = refs[:peers]
-    sums_ref = refs[peers]
-    recv_refs = refs[peers + 1 : 2 * peers + 1]
-    exp_ref = refs[2 * peers + 1]
-    parts, near_s, near_r, red_s, red_r, grp_s, grp_r, mem_s, mem_r = refs[2 * peers + 2 :]
+def sweep_kernel(peers, per_shell, n_grp, n_mem, *refs):
+    coef_ref, rot_ref, send_ref, clus_ref = refs[:4]
+    coup_ref, axial_ref, up_ref, far_ref, rott_ref, mie_ref, inc_ref = refs[4:11]
+    gid_ref, crot_ref, pcol_ref, prot_ref, out_ref = refs[11:16]
+    pool_ref, sums_ref, sent_ref, send_sel, got_ref, exp_ref, flat_ref = refs[16:23]
+    recv_s, count_s, sel_s, taken_s, far_s, gath_s, parts = refs[23:30]
+    near_s, near_r, red_s, red_r, grp_s, grp_r, mem_s, mem_r = refs[30:]
+    width = sent_ref.shape[1]
+    out_refs = [sent_ref.at[p] for p in range(peers)]
+    recv_refs = [got_ref.at[p] for p in range(peers)]
     g = lax.axis_index("grp")
     m = lax.axis_index("mem")
 
@@ -42,6 +46,10 @@
     barrier = pltpu.get_barrier_semaphore()
     for device in everyone:
         pl.semaphore_signal(barrier, inc=1, device_id=device, device_id_type=MESH)
+    rotate_columns(
+        peers, width, coef_ref, rot_ref, send_ref, clus_ref, crot_ref,
+        pool_ref, sums_ref, out_refs, send_sel,
+    )
     pl.semaphore_wait(barrier, len(everyone))
 
     reduce_copies = []
@@ -77,10 +85,17 @@
     ]
     for c in mem_copies:
         c.start()
+    rot_of = count_slots(peers, per_shell, sent_ref, pool_ref, inc_ref, pcol_ref, prot_ref, count_s, sel_s)
     for c in near_copies + mem_copies:
         c.wait_recv()
     for c in reduce_copies + near_copies + grp_copies + mem_copies:
         c.wait_send()
+    gather_columns(
+        peers, per_shell, rot_of, pool_ref, exp_ref, flat_ref, recv_refs,
+        coup_ref, axial_ref, up_ref, far_ref, rott_ref, mie_ref, inc_ref,
+        gid_ref, crot_ref, pcol_ref, out_ref,
+        recv_s, count_s, sel_s, taken_s, far_s, gath_s,
+    )
 
 
 def pair_apply(pair, wide):
@@ -104,10 +119,9 @@
     return lax.dot_general(a, b, (((1,), (1,)), ((), ())), preferred_element_type=F32)
 
 
-def rotate_kernel(peers, width, coef_ref, rot_ref, send_ref, clus_ref, crot_ref, *rest):
-    pool_ref, sums_ref = rest[0], rest[1]
-    out_refs = rest[2 : 2 + peers]
-    sel = rest[2 + peers]
+def rotate_columns(
+    peers, width, coef_ref, rot_ref, send_ref, clus_ref, crot_ref, pool_ref, sums_ref, out_refs, sel
+):
     comps, n_coef, sph = coef_ref.shape
     rots = rot_ref.shape[0]
     pool = rots * sph
@@ -139,19 +153,37 @@
             sums_ref[q, :, at : at + step] = picked[row : row + each]
 
 
-def gather_kernel(
-    peers,
-    per_shell,
-    pool_ref,
-    exp_ref,
-    *rest,
+def count_slots(peers, per_shell, sent_ref, pool_ref, inc_ref, pcol_ref, prot_ref, count_s, sel_s):
+    sph = inc_ref.shape[2]
+    shells = pcol_ref.shape[0] // per_shell
+    pool = pool_ref.shape[1]
+    total = peers * sent_ref.shape[1]
+    q_iota = lax.broadcasted_iota(jnp.int32, (total, sph), 0) + pool
+    rot_of = jnp.full((total, sph), -1.0, F32)
+    for h in range(shells):
+        count = jnp.zeros((total, sph), F32)
+        for s in range(h * per_shell, (h + 1) * per_shell):
+            hit = pcol_ref[s : s + 1, :] == q_iota
+            count = count + jnp.where(hit, 1.0, 0.0)
+            rot_of = jnp.where(hit, prot_ref[s : s + 1, :].astype(F32), rot_of)
+        count_s[:, h * sph : (h + 1) * sph] = count.astype(BF16)
+    rot_of = jnp.max(rot_of, axis=1, keepdims=True)
+    j_iota = lax.broadcasted_iota(jnp.int32, (sph, sph), 0)
+    for r in range(pool // sph):
+        for h in range(shells):
+            count = jnp.zeros((sph, sph), F32)
+            for s in range(h * per_shell, (h + 1) * per_shell):
+                count = count + jnp.where(pcol_ref[s : s + 1, :] == j_iota + r * sph, 1.0, 0.0)
+            sel_s[r, :, h * sph : (h + 1) * sph] = count.astype(BF16)
+    return rot_of
+
+
+def gather_columns(
+    peers, per_shell, rot_of, pool_ref, exp_ref, flat_ref, recv_refs,
+    coup_ref, axial_ref, up_ref, far_ref, rott_ref, mie_ref, inc_ref,
+    gid_ref, crot_ref, pcol_ref, out_ref,
+    recv_s, count_s, sel_s, taken_s, far_s, gath_s,
 ):
-    recv_refs = rest[:peers]
-    (
-        coup_ref, axial_ref, up_ref, far_ref, rott_ref, mie_ref, inc_ref,
-        gid_ref, crot_ref, pcol_ref, prot_ref, out_ref,
-        recv_s, count_s, sel_s, taken_s, far_s, gath_s,
-    ) = rest[peers:]
     comps, n_coef, sph = inc_ref.shape
     dirs = comps // 2
     slots = pcol_ref.shape[0]
@@ -166,22 +198,16 @@
     arrived = jnp.concatenate([recv_refs[p][...] for p in range(peers)], axis=0)
     recv_s[...] = arrived.T
 
-    q_iota = lax.broadcasted_iota(jnp.int32, (total, sph), 0) + pool
-    rot_of = jnp.full((total, sph), -1.0, F32)
-    for h in range(shells):
-        count = jnp.zeros((total, sph), F32)
-        for s in range(h * per_shell, (h + 1) * per_shell):
-            hit = pcol_ref[s : s + 1, :] == q_iota
-            count = count + jnp.where(hit, 1.0, 0.0)
-            rot_of = jnp.where(hit, prot_ref[s : s + 1, :].astype(F32), rot_of)
-        count_s[:, h * sph : (h + 1) * sph] = count.astype(BF16)
-    rot_of = jnp.max(rot_of, axis=1, keepdims=True)
-
     clus_iota = lax.broadcasted_iota(jnp.int32, (clus, sph), 0)
+    n_mem, n_grp, each = exp_ref.shape[0], exp_ref.shape[1], exp_ref.shape[2]
+    for a in range(n_mem):
+        for b in range(n_grp):
+            row = (a * n_grp + b) * each
+            flat_ref[row : row + each, :] = exp_ref[a, b]
     member = jnp.where(gid_ref[...] == clus_iota, 1.0, 0.0).astype(F32)
     weights = jnp.dot(coup_ref[...], member, precision=lax.Precision.HIGHEST, preferred_element_type=F32)
     near_sum = jnp.dot(
-        exp_ref[...].T, weights, precision=lax.Precision.HIGHEST, preferred_element_type=F32
+        flat_ref[...].T, weights, precision=lax.Precision.HIGHEST, preferred_element_type=F32
     )
     folded = jnp.concatenate(
         [near_sum[x * n_coef : (x + 1) * n_coef] for x in range(comps)], axis=1
@@ -195,20 +221,12 @@
     far_s[:, :half] = far_re
     far_s[:, half:] = far_im
 
-    j_iota = lax.broadcasted_iota(jnp.int32, (sph, sph), 0)
-
     @pl.loop(0, rots)
     def _(r):
         first = pl.multiple_of(r * sph, sph)
-        ids = j_iota + r * sph
-        for h in range(shells):
-            count = jnp.zeros((sph, sph), F32)
-            for s in range(h * per_shell, (h + 1) * per_shell):
-                count = count + jnp.where(pcol_ref[s : s + 1, :] == ids, 1.0, 0.0)
-            sel_s[:sph, h * sph : (h + 1) * sph] = count.astype(BF16)
         mine = rot_of == r.astype(F32)
-        sel_s[sph:, :] = jnp.where(mine, count_s[...].astype(F32), 0.0).astype(BF16)
-        sel = sel_s[...]
+        kept = jnp.where(mine, count_s[...].astype(F32), 0.0).astype(BF16)
+        sel = jnp.concatenate([sel_s[r], kept], axis=0)
         for x in range(comps):
             rows = slice(x * n_coef, (x + 1) * n_coef)
             lhs = jnp.concatenate([pool_ref[rows, pl.ds(first, sph)], recv_s[rows, :]], axis=1)
@@ -264,63 +282,44 @@
     clus_row = cluster_ids.reshape(1, sph)
     crot_row = center_rot.reshape(1, sph)
 
-    first = pl.pallas_call(
-        functools.partial(rotate_kernel, peers, width),
-        out_shape=[
-            jax.ShapeDtypeStruct((rows, pool), BF16),
-            jax.ShapeDtypeStruct((n_mem, each, rows), F32),
+    rott = jnp.transpose(rot_table, (2, 0, 1)).reshape(n_coef, rots * n_coef)
+    eye = jnp.arange(clus)[:, None] == jnp.arange(clus)[None, :]
+    coup_t = jnp.where(eye, F32(0.0), coupling).T
+    coup_t = coup_t.reshape(n_grp, n_mem, each, clus).transpose(1, 0, 2, 3).reshape(clus, clus)
+    gid = clus_row + lax.axis_index("grp") * group
+    dma = pltpu.SemaphoreType.DMA
+    return pl.pallas_call(
+        functools.partial(sweep_kernel, peers, per_shell, n_grp, n_mem),
+        out_shape=jax.ShapeDtypeStruct((comps, n_coef, sph), F32),
+        in_specs=[vmem] * 15,
+        out_specs=vmem,
+        scratch_shapes=[
+            pltpu.VMEM((rows, pool), BF16),
+            pltpu.VMEM((n_mem, each, rows), F32),
+            pltpu.VMEM((peers, width, rows), BF16),
+            pltpu.VMEM((total + group, pool), BF16),
+            pltpu.VMEM((peers, width, rows), BF16),
+            pltpu.VMEM((n_mem, n_grp, each, rows), F32),
+            pltpu.VMEM((clus, rows), F32),
+            pltpu.VMEM((rows, total), BF16),
+            pltpu.VMEM((total, shells * sph), BF16),
+            pltpu.VMEM((rots, sph, shells * sph), BF16),
+            pltpu.VMEM((shells, n_coef, comps * sph), BF16),
+            pltpu.VMEM((n_coef, comps * sph), F32),
+            pltpu.VMEM((rots, n_coef, comps * sph), BF16),
+            pltpu.VMEM((n_mem - 1, each, rows), F32),
         ]
-        + [jax.ShapeDtypeStruct((width, rows), BF16)] * peers,
-        in_specs=[vmem] * 5,
-        out_specs=[vmem] * (2 + peers),
-        scratch_shapes=[pltpu.VMEM((total + group, pool), BF16)],
-        compiler_params=pltpu.CompilerParams(vmem_limit_bytes=40 * MIB),
-        name="rotate",
-    )(coefficients, rot_table, send_col.reshape(total, 1), clus_row, crot_row)
-    rotated, sums = first[0], first[1]
-    outgoing = first[2:]
-    dma = pltpu.SemaphoreType.DMA
-    exchanged = pl.pallas_call(
-        functools.partial(exchange_kernel, peers, n_grp, n_mem),
-        out_shape=[jax.ShapeDtypeStruct((width, rows), BF16)] * peers
-        + [jax.ShapeDtypeStruct((n_mem, n_grp, each, rows), F32)],
-        in_specs=[vmem] * (peers + 1),
-        out_specs=[vmem] * (peers + 1),
-        scratch_shapes=[pltpu.VMEM((n_mem - 1, each, rows), F32)]
         + [dma((peers,))] * 2
         + [dma((n_mem - 1,))] * 2
         + [dma((n_grp - 1,))] * 2
         + [dma((n_mem - 1,))] * 2,
         compiler_params=pltpu.CompilerParams(
-            collective_id=0, has_side_effects=True, vmem_limit_bytes=32 * MIB
+            collective_id=0, has_side_effects=True, vmem_limit_bytes=52 * MIB
         ),
-        name="exchange",
-    )(*outgoing, sums)
-    received = exchanged[:peers]
-    expansions = exchanged[peers].reshape(clus, rows)
-
-    rott = jnp.transpose(rot_table, (2, 0, 1)).reshape(n_coef, rots * n_coef)
-    eye = jnp.arange(clus)[:, None] == jnp.arange(clus)[None, :]
-    coup_t = jnp.where(eye, F32(0.0), coupling).T
-    coup_t = coup_t.reshape(n_grp, n_mem, each, clus).transpose(1, 0, 2, 3).reshape(clus, clus)
-    gid = clus_row + lax.axis_index("grp") * group
-    return pl.pallas_call(
-        functools.partial(gather_kernel, peers, per_shell),
-        out_shape=jax.ShapeDtypeStruct((comps, n_coef, sph), F32),
-        in_specs=[vmem] * (13 + peers),
-        out_specs=vmem,
-        scratch_shapes=[
-            pltpu.VMEM((rows, total), BF16),
-            pltpu.VMEM((total, shells * sph), BF16),
-            pltpu.VMEM((sph + total, shells * sph), BF16),
-            pltpu.VMEM((shells, n_coef, comps * sph), BF16),
-            pltpu.VMEM((n_coef, comps * sph), F32),
-            pltpu.VMEM((rots, n_coef, comps * sph), BF16),
-        ],
-        compiler_params=pltpu.CompilerParams(vmem_limit_bytes=48 * MIB),
-        name="gather",
+        name="sweep",
     )(
-        rotated, expansions, *received, coup_t, axial_shells, up_axial, far_axial, rott, mie_coeffs.T, incident,
+        coefficients, rot_table, send_col.reshape(total, 1), clus_row,
+        coup_t, axial_shells, up_axial, far_axial, rott, mie_coeffs.T, incident,
         gid, crot_row, pair_col, pair_rot,
     )
 

time: 85.2 us -> 67.3 us (0.79); the launches traced: 83.7 us -> 67 us
  local copies, waits for them, and re-layouts: 20.7 us -> 7.55 us
  Pallas kernels: 62.8 us -> 59.3 us
    unnamed x58 -> x21, local copies, waits for them, and re-layouts: 18.7 us -> 5.07 us
    pallas_call x3 -> x1, Pallas kernels: 62.8 us -> 59.3 us  [on_device(): pl.pallas_call(functools.partial(sweep_kernel, peers, per_shell, n_grp, n...]
    reshape x1, local copies, waits for them, and re-layouts: 0.85 us -> 2.31 us  [on_device(): rott = jnp.transpose(rot_table, (2, 0, 1)).reshape(n_coef, rots * n_coef)]
where the time goes in v3:
time: 67.3 us; the launch traced here: 67 us
  Pallas kernels  59.3 us (88%)
  local copies, waits for them, and re-layouts  7.55 us (11%)
    pallas_call x1, Pallas kernels, on_device(): pl.pallas_call(functools.partial(sweep_kernel, peers, per_shell, n_grp, n...  59.3 us
    unnamed x21, local copies, waits for them, and re-layouts  5.07 us
    reshape x1, local copies, waits for them, and re-layouts, on_device(): rott = jnp.transpose(rot_table, (2, 0, 1)).reshape(n_coef, rots * n_coef)  2.31 us

profile of v3, /device:TPU:0, one launch (start us, length us, event | category | flops | bytes accessed | tf_op | source)
XLA Modules:
  0.0 67.0 jit_solution(14294997482490332989)
XLA Ops:
  0.0 0.0 copy-start.5
  0.0 0.7 copy-done.5
  0.7 0.8 %copy.17 = f32[64,64]{0,1:T(8,128)S(1)} copy(f32[64,64]{1,0:T(8,128)} %param.20) | data formatting | bytes 32768 | tf_op args[7]
  1.5 0.0 copy-start.8
  1.5 0.7 copy-done.8
  2.2 0.0 copy-start.7
  2.2 0.1 copy.20
  2.3 0.5 copy-done.7
  2.9 0.2 reshape.25.refs_2_
  3.1 0.0 copy-start
  3.1 0.0 copy-start.1
  3.1 0.0 copy-start.2
  3.1 0.0 copy-start.3
  3.1 0.0 copy-start.4
  3.1 0.0 copy-start.6
  3.1 2.3 %copy.22.refs_8_ = bf16[240,1920]{1,0:T(8,128)(2,1)} copy(bf16[240,1920]{0,1:T(8,128)(2,1)} %bitcast.18) | data formatting | bytes 1843200 | tf_op jit(solution)/shard_map/reshape | solution.py:285
  5.4 0.0 copy-done
  5.4 0.0 copy-done.1
  5.4 0.0 copy-done.2
  5.4 0.0 copy-done.3
  5.5 0.0 copy-done.4
  5.5 0.0 copy-done.6
  5.5 59.3 %sweep.1 = f32[8,240,128]{2,1,0:T(8,128)} custom-call(f32[8,240,128]{2,1,0:T(8,128)} %refs_0_.1, bf16[8,240,240]{2,1,0:T(8,128)(2,1)} %refs_1_.1, s32[384,1]{1,0:T(8,128)S(1)} %reshape.25.refs_2_, s32[1,128]{1,0:T(1,128)S(1)} %bitcast.16, f32[64,64]{1,0:T(8,128)S(1)} %bitcast.15, bf16[3,2,240,240]{3,2,1,0:T(8,128)(2,1)S(1)} %copy-done, ...), custom_call_target="tpu_custom_call" | custom-call | tf_op jit(solution)/shard_map/sweep/pallas_call | solution.py:291
  64.8 2.2 %copy.24 = f32[8,240,128]{2,1,0:T(8,128)} copy(f32[8,240,128]{2,1,0:T(8,128)} %sweep.1) | data formatting | bytes 1966080
  (3 shorter events, 0.0 us)
Async XLA Ops:
  0.0 0.7 copy-start.5
  1.5 0.7 %copy-start.8 = (f32[2,240]{1,0:T(2,128)S(1)}, f32[2,240]{1,0:T(2,128)}, u32[]{:S(2)}) copy-start(f32[2,240]{1,0:T(2,128)} %param.15) | copy-start | bytes 5764
  2.2 0.7 %copy-start.7 = (s32[6,64]{1,0:T(8,128)S(1)}, s32[6,64]{1,0:T(8,128)}, u32[]{:S(2)}) copy-start(s32[6,64]{1,0:T(8,128)} %param.25) | copy-start | bytes 4612
  3.1 2.4 %copy-start = (bf16[3,2,240,240]{3,2,1,0:T(8,128)(2,1)S(1)}, bf16[3,2,240,240]{3,2,1,0:T(8,128)(2,1)}, u32[]{:S(2)}) copy-start(bf16[3,2,240,240]{3,2,1,0:T(8,128)(2,1)} %refs_5_.1) | copy-start | bytes 2073604
  3.1 2.4 %copy-start.1 = (bf16[2,240,240]{2,1,0:T(8,128)(2,1)S(1)}, bf16[2,240,240]{2,1,0:T(8,128)(2,1)}, u32[]{:S(2)}) copy-start(bf16[2,240,240]{2,1,0:T(8,128)(2,1)} %refs_6_.1) | copy-start | bytes 691204
  3.1 2.4 %copy-start.2 = (bf16[2,240,240]{2,1,0:T(8,128)(2,1)S(1)}, bf16[2,240,240]{2,1,0:T(8,128)(2,1)}, u32[]{:S(2)}) copy-start(bf16[2,240,240]{2,1,0:T(8,128)(2,1)} %refs_7_.1) | copy-start | bytes 691204
  3.1 2.4 %copy-start.3 = (s32[24,128]{1,0:T(8,128)S(1)}, s32[24,128]{1,0:T(8,128)}, u32[]{:S(2)}) copy-start(s32[24,128]{1,0:T(8,128)} %refs_13_.1) | copy-start | bytes 36868
  3.1 2.4 %copy-start.4 = (s32[24,128]{1,0:T(8,128)S(1)}, s32[24,128]{1,0:T(8,128)}, u32[]{:S(2)}) copy-start(s32[24,128]{1,0:T(8,128)} %refs_14_.1) | copy-start | bytes 36868
  3.1 2.4 %copy-start.6 = (s32[128]{0:T(128)S(1)}, s32[128]{0:T(128)}, u32[]{:S(2)}) copy-start(s32[128]{0:T(128)} %param.22) | copy-start | bytes 1540
